TPU v7x, 32 devices: a whole 2x2x4 slice. The times are simulated.
32 devices in a mesh: dp: 2 (over x), blk: 4 (over z), tensor: 4 (over y, core).
Axes of the slice: x: 2, y: 2, z: 4, core: 2. Of those that a mesh axis runs over, the one named last changes fastest.
Arguments:
- block_input: bfloat16 [4, 2048, 2048], P('dp', 'blk', 'tensor'), may hold values from -6 to 6
- segment_ids: int32 [4, 2048], P('dp'), may hold values from 0 to 7, as said below
- layer_norm_gain: float32 [2048], replicated, may hold values from 0.5 to 1.5
- layer_norm_bias: float32 [2048], replicated, may hold values from -4 to 4
- qkv_weight: bfloat16 [2048, 3, 2048], P(None, None, 'tensor'), may hold values from -0.125 to 0.125
- qkv_bias: float32 [3, 2048], P(None, 'tensor'), may hold values from -0.4375 to 0.4375
- out_weight: bfloat16 [2048, 2048], P('tensor'), may hold values from -2 to 2
- out_bias: float32 [2048], P('tensor'), may hold values from -4 to 4
- up_weight: bfloat16 [2048, 8192], P(None, 'tensor'), may hold values from -0.125 to 0.125
- up_bias: float32 [8192], P('tensor'), may hold values from -4 to 4
- down_weight: bfloat16 [8192, 2048], P('tensor'), may hold values from -0.0625 to 0.0625
- down_bias: float32 [2048], P('tensor'), may hold values from -4 to 4
- grad_output: bfloat16 [4, 2048, 2048], P('dp', 'blk', 'tensor'), may hold values from -6 to 6
Outputs:
- block_output: bfloat16 [4, 2048, 2048], P('dp', 'blk', 'tensor')
- input_grad: bfloat16 [4, 2048, 2048], P('dp', 'blk', 'tensor')
- norm_gain_grad: float32 [2048], P('tensor')
- norm_bias_grad: float32 [2048], P('tensor')
- qkv_weight_grad: float32 [2048, 3, 2048], P(None, None, 'tensor')
- qkv_bias_grad: float32 [3, 2048], P(None, 'tensor')
- out_weight_grad: float32 [2048, 2048], P('tensor')
- out_bias_grad: float32 [2048], P('tensor')
- up_weight_grad: float32 [2048, 8192], P(None, 'tensor')
- up_bias_grad: float32 [8192], P('tensor')
- down_weight_grad: float32 [8192, 2048], P('tensor')
- down_bias_grad: float32 [2048], P('tensor')
Inputs may be any that keep to these rules, and one draw needn't show every extreme that they name: `segment_ids`: segment ids never fall along a row; each row uses every id from 0 to 7, and in each row one document holds every position from 256 to 1792.
All inputs are finite; a program needn't handle non-finite values.
Results may differ from a plain program's by a relative error of at most 0.02.
Values may be sent and summed in bfloat16 or wider, within the bound.
A program may use at most 320 MiB of HBM per device.

v0:
```python
from functools import partial
import math

import jax
import jax.numpy as jnp
from jax import lax
from jax.sharding import PartitionSpec as P

HD = 64
ROT = 32


EPSILON = 1e-05
ROPE_LOG_BASE = math.log(10000.0)
NEGATIVE = -1e30


def document_offsets(segment_ids):
    places = jnp.arange(segment_ids.shape[1])
    changed = jnp.concatenate(
        [
            jnp.ones((segment_ids.shape[0], 1), dtype=bool),
            segment_ids[:, 1:] != segment_ids[:, :-1],
        ],
        axis=1,
    )
    starts = lax.cummax(jnp.where(changed, places[None, :], jnp.zeros_like(segment_ids)), axis=1)
    return (places[None, :] - starts).astype(jnp.float32)


def rotary_tables(positions):
    half_rot = ROT // 2
    steps_float = jnp.arange(half_rot).astype(jnp.float32)
    inverse_freq = jnp.exp(steps_float * (-2.0 / ROT) * ROPE_LOG_BASE)
    angles = positions[..., None] * inverse_freq
    return (jnp.cos(angles), jnp.sin(angles))


def rotate(source, cos_t, sin_t):
    half_rot = ROT // 2
    front_half = source[..., :half_rot]
    back_half = source[..., half_rot:ROT]
    cos_b = cos_t[..., None, :]
    sin_b = sin_t[..., None, :]
    return jnp.concatenate(
        [
            front_half * cos_b - back_half * sin_b,
            back_half * cos_b + front_half * sin_b,
            source[..., ROT:],
        ],
        axis=-1,
    )


def masked_scores(query_row, key_row, query_segment, key_segment, query_places, score_scale):
    scores = (
        jnp.einsum("qhd,khd->hqk", query_row, key_row, preferred_element_type=jnp.float32)
        * score_scale
    )
    key_places = jnp.arange(key_segment.shape[0])
    allowed = (query_segment[:, None] == key_segment[None, :]) & (
        query_places[:, None] >= key_places[None, :]
    )
    return jnp.where(allowed[None], scores, NEGATIVE)


def local(
    block_input,
    segment_ids,
    layer_norm_gain,
    layer_norm_bias,
    qkv_weight,
    qkv_bias,
    out_weight,
    out_bias,
    up_weight,
    up_bias,
    down_weight,
    down_bias,
    grad_output,
):
    row_count, block_len, feature_slice_width = block_input.shape
    local_width = qkv_weight.shape[2]
    heads_here = local_width // HD
    score_scale = HD ** (-0.5)
    cycle_index = lax.axis_index("blk")
    tensor_index = lax.axis_index("tensor")
    full_input, full_grad = (
        lax.all_gather(block_input, "tensor", axis=2, tiled=True),
        lax.all_gather(grad_output, "tensor", axis=2, tiled=True),
    )
    input_float = full_input.astype(jnp.float32)
    row_mean = jnp.mean(input_float, axis=-1, keepdims=True)
    mean_centered = input_float - row_mean
    variance = jnp.mean(mean_centered * mean_centered, axis=-1, keepdims=True)
    inverse_stddev = lax.rsqrt(variance + EPSILON)
    standardized_input = mean_centered * inverse_stddev
    normalized_rows = (standardized_input * layer_norm_gain + layer_norm_bias).astype(jnp.bfloat16)
    qkv_all = (
        jnp.einsum("rcd,dke->rcke", normalized_rows, qkv_weight, preferred_element_type=jnp.float32)
        + qkv_bias
    )
    qkv_split = qkv_all.reshape(row_count, block_len, 3, heads_here, HD)
    query_places = cycle_index * block_len + jnp.arange(block_len)
    offsets_here = lax.dynamic_slice_in_dim(
        document_offsets(segment_ids), cycle_index * block_len, block_len, 1
    )
    cos_t, sin_t = rotary_tables(offsets_here)
    queries = rotate(qkv_split[:, :, 0], cos_t, sin_t).astype(jnp.bfloat16)
    keys_here = (
        rotate(qkv_split[:, :, 1], cos_t, sin_t)
        .astype(jnp.bfloat16)
        .reshape(row_count, block_len, local_width)
    )
    values_here = qkv_split[:, :, 2].astype(jnp.bfloat16).reshape(row_count, block_len, local_width)
    all_keys, all_values = (
        lax.all_gather(keys_here, "blk", axis=1, tiled=True),
        lax.all_gather(values_here, "blk", axis=1, tiled=True),
    )
    length = all_keys.shape[1]
    all_keys = all_keys.reshape(row_count, length, heads_here, HD)
    all_values = all_values.reshape(row_count, length, heads_here, HD)
    query_segments = lax.dynamic_slice_in_dim(segment_ids, cycle_index * block_len, block_len, 1)

    def forward_row(row_items):
        query_row, key_row, value_row, query_segment, key_segment = row_items
        scores = masked_scores(
            query_row, key_row, query_segment, key_segment, query_places, score_scale
        )
        row_top = jnp.max(scores, axis=-1, keepdims=True)
        expo = jnp.exp(scores - row_top)
        row_total = jnp.sum(expo, axis=-1, keepdims=True)
        attn_probs = (expo / row_total).astype(jnp.bfloat16)
        mixed = jnp.einsum(
            "hqk,khd->qhd", attn_probs, value_row, preferred_element_type=jnp.float32
        )
        return (mixed, row_top, row_total)

    mixed_all, row_tops, row_totals = lax.map(
        forward_row, (queries, all_keys, all_values, query_segments, segment_ids)
    )
    attended = mixed_all.astype(jnp.bfloat16).reshape(row_count, block_len, local_width)
    hidden = (
        jnp.einsum("rcd,df->rcf", normalized_rows, up_weight, preferred_element_type=jnp.float32)
        + up_bias
    )
    active, gelu_back = jax.vjp(partial(jax.nn.gelu, approximate=True), hidden)
    active_low = active.astype(jnp.bfloat16)
    partial_sum = jnp.einsum(
        "rce,ed->rcd", attended, out_weight, preferred_element_type=jnp.float32
    )
    partial_sum = partial_sum + jnp.einsum(
        "rcf,fd->rcd", active_low, down_weight, preferred_element_type=jnp.float32
    )
    branch = lax.psum_scatter(partial_sum, "tensor", scatter_dimension=2, tiled=True)
    block_output = (block_input.astype(jnp.float32) + (branch + out_bias + down_bias)).astype(
        jnp.bfloat16
    )
    grad_share = grad_output.astype(jnp.float32)
    bias_grad = jnp.sum(grad_share, axis=(0, 1))
    out_weight_grad = jnp.einsum(
        "rce,rcd->ed", attended, full_grad, preferred_element_type=jnp.float32
    )
    down_weight_grad = jnp.einsum(
        "rcf,rcd->fd", active_low, full_grad, preferred_element_type=jnp.float32
    )
    grad_attended = jnp.einsum(
        "rcd,ed->rce", full_grad, out_weight, preferred_element_type=jnp.float32
    ).astype(jnp.bfloat16)
    grad_attended = grad_attended.reshape(row_count, block_len, heads_here, HD)
    grad_active = jnp.einsum(
        "rcd,fd->rcf", full_grad, down_weight, preferred_element_type=jnp.float32
    )
    grad_hidden = gelu_back(grad_active)[0].astype(jnp.bfloat16)
    up_bias_grad = jnp.sum(grad_hidden.astype(jnp.float32), axis=(0, 1))
    up_weight_grad = jnp.einsum(
        "rcd,rcf->df", normalized_rows, grad_hidden, preferred_element_type=jnp.float32
    )

    def backward_row(row_items):
        query_row, key_row, value_row, query_segment, key_segment, grad_row, row_top, row_total = (
            row_items
        )
        scores = masked_scores(
            query_row, key_row, query_segment, key_segment, query_places, score_scale
        )
        probs_exact = jnp.exp(scores - row_top) / row_total
        probs_low = probs_exact.astype(jnp.bfloat16)
        grad_probs = jnp.einsum(
            "qhd,khd->hqk", grad_row, value_row, preferred_element_type=jnp.float32
        )
        delta_row = jnp.sum(probs_exact * grad_probs, axis=-1, keepdims=True)
        grad_scores = (probs_exact * (grad_probs - delta_row)).astype(jnp.bfloat16)
        grad_query = (
            jnp.einsum("hqk,khd->qhd", grad_scores, key_row, preferred_element_type=jnp.float32)
            * score_scale
        )
        grad_key = (
            jnp.einsum("hqk,qhd->khd", grad_scores, query_row, preferred_element_type=jnp.float32)
            * score_scale
        )
        grad_value = jnp.einsum(
            "hqk,qhd->khd", probs_low, grad_row, preferred_element_type=jnp.float32
        )
        return (grad_query, grad_key, grad_value)

    grad_queries, grad_keys, grad_values = lax.map(
        backward_row,
        (
            queries,
            all_keys,
            all_values,
            query_segments,
            segment_ids,
            grad_attended,
            row_tops,
            row_totals,
        ),
    )
    key_sum, value_sum = (
        lax.psum_scatter(
            grad_keys.reshape(row_count, length, local_width),
            "blk",
            scatter_dimension=1,
            tiled=True,
        ),
        lax.psum_scatter(
            grad_values.reshape(row_count, length, local_width),
            "blk",
            scatter_dimension=1,
            tiled=True,
        ),
    )
    query_back = rotate(grad_queries, cos_t, -sin_t)
    key_back = rotate(key_sum.reshape(row_count, block_len, heads_here, HD), cos_t, -sin_t)
    value_back = value_sum.reshape(row_count, block_len, heads_here, HD)
    grad_qkv = (
        jnp.stack([query_back, key_back, value_back], axis=2)
        .reshape(row_count, block_len, 3, local_width)
        .astype(jnp.bfloat16)
    )
    qkv_bias_grad = jnp.sum(grad_qkv.astype(jnp.float32), axis=(0, 1))
    qkv_weight_grad = jnp.einsum(
        "rcd,rcke->dke", normalized_rows, grad_qkv, preferred_element_type=jnp.float32
    )
    grad_normed = jnp.einsum(
        "rcke,dke->rcd", grad_qkv, qkv_weight, preferred_element_type=jnp.float32
    )
    grad_normed = grad_normed + jnp.einsum(
        "rcf,df->rcd", grad_hidden, up_weight, preferred_element_type=jnp.float32
    )
    slice_offset = tensor_index * feature_slice_width
    gradient_complete = lax.psum(grad_normed, "tensor")
    gain_scaled = gradient_complete * layer_norm_gain
    first_moment = jnp.mean(gain_scaled, axis=-1, keepdims=True)
    second_moment = jnp.mean(gain_scaled * standardized_input, axis=-1, keepdims=True)
    input_complete = inverse_stddev * (
        gain_scaled - first_moment - standardized_input * second_moment
    )
    grad_input = lax.dynamic_slice_in_dim(input_complete, slice_offset, feature_slice_width, 2)
    gain_grad = lax.dynamic_slice_in_dim(
        jnp.sum(gradient_complete * standardized_input, axis=(0, 1)),
        slice_offset,
        feature_slice_width,
        0,
    )
    shift_grad = lax.dynamic_slice_in_dim(
        jnp.sum(gradient_complete, axis=(0, 1)), slice_offset, feature_slice_width, 0
    )
    input_grad = (grad_share + grad_input).astype(jnp.bfloat16)
    summed = (
        lax.psum(gain_grad.astype(jnp.bfloat16), ("dp", "blk")).astype(jnp.float32),
        lax.psum(shift_grad.astype(jnp.bfloat16), ("dp", "blk")).astype(jnp.float32),
        lax.psum(qkv_weight_grad.astype(jnp.bfloat16), ("dp", "blk")).astype(jnp.float32),
        lax.psum(qkv_bias_grad.astype(jnp.bfloat16), ("dp", "blk")).astype(jnp.float32),
        lax.psum(out_weight_grad.astype(jnp.bfloat16), ("dp", "blk")).astype(jnp.float32),
        lax.psum(bias_grad.astype(jnp.bfloat16), ("dp", "blk")).astype(jnp.float32),
        lax.psum(up_weight_grad.astype(jnp.bfloat16), ("dp", "blk")).astype(jnp.float32),
        lax.psum(up_bias_grad.astype(jnp.bfloat16), ("dp", "blk")).astype(jnp.float32),
        lax.psum(down_weight_grad.astype(jnp.bfloat16), ("dp", "blk")).astype(jnp.float32),
    )
    return (
        block_output,
        input_grad,
        summed[0],
        summed[1],
        summed[2],
        summed[3],
        summed[4],
        summed[5],
        summed[6],
        summed[7],
        summed[8],
        summed[5],
    )


def solution(mesh):
    in_specs = (
        P("dp", "blk", "tensor"),
        P("dp", None),
        P(),
        P(),
        P(None, None, "tensor"),
        P(None, "tensor"),
        P("tensor", None),
        P("tensor"),
        P(None, "tensor"),
        P("tensor"),
        P("tensor", None),
        P("tensor"),
        P("dp", "blk", "tensor"),
    )
    out_specs = (
        P("dp", "blk", "tensor"),
        P("dp", "blk", "tensor"),
        P("tensor"),
        P("tensor"),
        P(None, None, "tensor"),
        P(None, "tensor"),
        P("tensor", None),
        P("tensor"),
        P(None, "tensor"),
        P("tensor"),
        P("tensor", None),
        P("tensor"),
    )
    return jax.shard_map(local, mesh=mesh, in_specs=in_specs, out_specs=out_specs, check_vma=False)
```

profile of v0, /device:TPU:0, one launch (start us, length us, event | category | flops | bytes accessed | tf_op | source)
XLA Modules:
  0.0 1899.5 jit_solution(3413611991763300577)
XLA Ops:
  11.8 35.1 %all-gather.5.cloned.1.call-done = bf16[2,512,2048]{2,1,0:T(8,128)(2,1)} async-done(((bf16[2,512,512]{2,1,0:T(8,128)(2,1)}), bf16[2,512,2048]{2,1,0:T(8,128)(2,1)}) %all-gather.5.cloned.1.call-update) | async-done | bytes 4194320 | tf_op jit(solution)/shard_map/all_gather | solution.py:89
  49.8 3.4 fusion.62
  53.3 11.0 broadcast_add_fusion
  75.5 7.4 all-gather.11.cloned.1.call-done
  82.9 5.5 fusion.103
  88.5 77.4 %all-gather.9.cloned.1.call-done = bf16[2,2048,512]{1,2,0:T(8,128)(2,1)} async-done(((bf16[2,512,512]{1,2,0:T(8,128)(2,1)}), bf16[2,2048,512]{1,2,0:T(8,128)(2,1)}) %all-gather.9.cloned.1.call-update) | async-done | bytes 4194320 | tf_op jit(solution)/shard_map/all_gather | solution.py:117
  165.9 81.3 %all-gather.7.cloned.1.call-done = bf16[2,2048,512]{1,2,0:T(8,128)(2,1)} async-done(((bf16[2,512,512]{1,2,0:T(8,128)(2,1)}), bf16[2,2048,512]{1,2,0:T(8,128)(2,1)}) %all-gather.7.cloned.1.call-update) | async-done | bytes 4194320 | tf_op jit(solution)/shard_map/all_gather | solution.py:118
  247.2 93.9 %while.32 = (s32[]{:T(128)}, bf16[2,512,8,64]{1,3,2,0:T(8,128)(2,1)}, f32[2,8,512,1]{2,1,3,0:T(8,128)S(1)}, f32[2,8,512,1]{2,1,3,0:T(8,128)S(1)}, bf16[2,2048,8,...) while((s32[]{:T(128)}, ...), condition=%wide.region_7.8_spmd.clone.clone, body=%wide.region_4.7_spmd.clone.sunk.clone | while | flops 2251284992 | bytes 110809208 | solution.py:139
  248.4 15.1 fusion.157
  263.5 15.0 fusion.158
  278.5 15.6 fusion.159
  295.4 15.1 fusion.157
  310.5 15.0 fusion.158
  325.5 15.6 fusion.159
  341.1 234.9 %while.33 = (s32[]{:T(128)}, f32[2,512,8,64]{1,3,2,0:T(8,128)}, f32[2,2048,8,64]{1,3,2,0:T(8,128)}, f32[2,2048,8,64]{1,3,2,0:T(8,128)}, bf16[2,2048,8,64]{1,3,2,...) while((s32[]{:T(128)}, f32[2,512,8,64]{1,3,2,0:T(8,128)}, ...), condition=%wide.region_11.12_spmd.clone.clone, body=%wide.region_9.11_spmd.clone.sunk.clone | while | flops 5457048064 | bytes 296918208 | solution.py:207
  354.1 17.5 fusion.168
  371.6 26.2 %multiply_reduce_fusion.5 = (f32[8,512]{1,0:T(8,128)S(1)}, f32[8,512,2048]{2,1,0:T(8,128)}) fusion(f32[8,512,2048]{2,1,0:T(8,128)} %fusion.168, f32[8,512]{1,0:T(8,128)S(1)} %get-tuple-element.482, f32[8,512]{1,0:T(8,128)S(1)} %get-tuple-element.483, bf16[2,2048,8,64]{1,3,2,0:T(8,128)(2,1)S(1)} %copy-done.1, s32[]{:T(128)} %get-tuple-element.543, ...), kind=kOutput, calls=%fused_computation.29.clone.1.clone | convolution fusion | flops 1124069376 | bytes 70829056 | tf_op jit(solution)/shard_map/while/body/eval_jaxpr/qhd,khd->hqk/dot_general | solution.py:57
  397.8 27.4 %multiply_convert_fusion.6 = bf16[8,512,2048]{2,1,0:T(8,128)(2,1)} fusion(f32[8,512,2048]{2,1,0:T(8,128)} %get-tuple-element.484, f32[8,512,2048]{2,1,0:T(8,128)} %fusion.168, f32[8,512]{1,0:T(8,128)S(1)} %get-tuple-element.485), kind=kLoop, calls=%fused_computation.28.clone.1.clone | loop fusion | flops 25165824 | bytes 83902464 | tf_op jit(solution)/shard_map/while/body/eval_jaxpr/convert_element_type | solution.py:193
  425.2 10.8 bitcast_dynamic-update-slice_fusion.11
  436.0 12.7 fusion.170
  448.7 15.6 bitcast_dynamic-update-slice_fusion.12
  465.5 17.5 fusion.168
  483.1 26.2 %multiply_reduce_fusion.5 = (f32[8,512]{1,0:T(8,128)S(1)}, f32[8,512,2048]{2,1,0:T(8,128)}) fusion(f32[8,512,2048]{2,1,0:T(8,128)} %fusion.168, f32[8,512]{1,0:T(8,128)S(1)} %get-tuple-element.482, f32[8,512]{1,0:T(8,128)S(1)} %get-tuple-element.483, bf16[2,2048,8,64]{1,3,2,0:T(8,128)(2,1)S(1)} %copy-done.1, s32[]{:T(128)} %get-tuple-element.543, ...), kind=kOutput, calls=%fused_computation.29.clone.1.clone | convolution fusion | flops 1124069376 | bytes 70829056 | tf_op jit(solution)/shard_map/while/body/eval_jaxpr/qhd,khd->hqk/dot_general | solution.py:57
  509.2 27.4 %multiply_convert_fusion.6 = bf16[8,512,2048]{2,1,0:T(8,128)(2,1)} fusion(f32[8,512,2048]{2,1,0:T(8,128)} %get-tuple-element.484, f32[8,512,2048]{2,1,0:T(8,128)} %fusion.168, f32[8,512]{1,0:T(8,128)S(1)} %get-tuple-element.485), kind=kLoop, calls=%fused_computation.28.clone.1.clone | loop fusion | flops 25165824 | bytes 83902464 | tf_op jit(solution)/shard_map/while/body/eval_jaxpr/convert_element_type | solution.py:193
  536.6 10.8 bitcast_dynamic-update-slice_fusion.11
  547.4 12.7 fusion.170
  560.1 15.6 bitcast_dynamic-update-slice_fusion.12
  576.1 8.9 copy.40
  585.8 14.6 fusion.76
  602.8 17.7 fusion.86
  620.6 19.4 %fusion.112 = (bf16[2048]{0:T(1024)(128)(2,1)}, bf16[2,512,2048]{2,1,0:T(8,128)(2,1)S(1)}) fusion(f32[2,512,2048]{2,1,0:T(8,128)} %fusion.76, f32[2048]{0:T(1024)S(1)} %copy-done.28, bf16[2,512,2048]{2,1,0:T(8,128)(2,1)} %all-gather.11.cloned.1.call-done, bf16[2048,2048]{1,0:T(8,128)(2,1)} %param.27), kind=kOutput, calls=%fused_computation.162 | convolution fusion | flops 8636069888 | bytes 25178112 | tf_op jit(solution)/shard_map/rcd,fd->rcf/dot_general | solution.py:171
  640.1 13.5 fusion.74
  653.6 12.0 bitcast_convert_fusion.1
  665.6 12.4 bitcast_convert_fusion
  680.1 3.7 bitcast_convert_fusion.3
  683.8 35.4 %reduce-scatter.6.cloned.1.call-done = f32[2,512,512]{1,2,0:T(8,128)} async-done(((f32[2,2048,512]{1,2,0:T(8,128)}), f32[2,512,512]{1,2,0:T(8,128)}) %reduce-scatter.6.cloned.1.call-update) | async-done | bytes 2097168 | tf_op jit(solution)/shard_map/reduce_scatter | solution.py:221
  728.5 138.1 %reduce-scatter.8.cloned.1.call-done = f32[2,512,512]{2,1,0:T(8,128)} async-done(((f32[2,2048,512]{2,1,0:T(8,128)}), f32[2,512,512]{2,1,0:T(8,128)}) %reduce-scatter.8.cloned.1.call-update) | async-done | bytes 2097168 | tf_op jit(solution)/shard_map/reduce_scatter | solution.py:227
  868.4 13.4 bitcast_add_fusion
  881.9 13.8 bitcast_convert_fusion.2
  899.6 42.7 %reduce-scatter.4.cloned.1.call-done = f32[2,512,512]{2,1,0:T(8,128)} async-done(((f32[2,512,2048]{2,1,0:T(8,128)}), f32[2,512,512]{2,1,0:T(8,128)}) %reduce-scatter.4.cloned.1.call-update) | async-done | bytes 2097168 | tf_op jit(solution)/shard_map/reduce_scatter | solution.py:155
  945.5 152.9 %all-reduce.6.cloned.1.call-done = f32[2,512,2048]{2,1,0:T(8,128)} async-done(((f32[2,512,2048]{2,1,0:T(8,128)}), f32[2,512,2048]{2,1,0:T(8,128)}) %all-reduce.6.cloned.1.call-update) | async-done | bytes 8388624 | tf_op jit(solution)/shard_map/psum | solution.py:253
  1098.4 11.0 fusion.110
  1109.6 39.8 %all-reduce.1 = (bf16[512]{0:T(512)(128)(2,1)S(1)}, bf16[512]{0:T(512)(128)(2,1)S(1)}, bf16[3,512]{1,0:T(4,128)(2,1)S(1)}, bf16[512]{0:T(512)(128)(2,1)S(1)}, bf16[2048]{0:T(1024)(128)(2,1)S(1)}) all-reduce(bf16[512]{0:T(512)(128)(2,1)S(1)} %dynamic_slice.161, ...), channel_id=1, replica_groups=mesh['dp'=2,'blk'=4,'tensor'=4] {'dp','blk'}, use_global_device_ids=true, to_apply=%region_18.19 | all-reduce | flops 5120 | bytes 20480 | tf_op jit(solution)/shard_map/psum | solution.py:272
  1151.7 3.8 fusion.98
  1155.5 701.3 %all-reduce.8.cloned.1.call-done = (bf16[2048,3,512]{2,0,1:T(8,128)(2,1)}, bf16[512,2048]{1,0:T(8,128)(2,1)}, bf16[2048,2048]{1,0:T(8,128)(2,1)}, bf16[2048,2048]{1,0:T(8,128)(2,1)}) async-done(((bf16[2048,3,512]{2,0,1:T(8,128)(2,1)}, bf16[512,2048]{1,0:T(8,128)(2,1)}, bf16[2048,2048]{1,0:T(8,128)(2,1)}, bf16[2048,2048]{1,0:T(8,128)(2,1)}), (bf16[2048,3,512]{2,0,1:T(8,128)(2,1)}, ...) | async-done | bytes 25165840 | tf_op jit(solution)/shard_map/psum | solution.py:274
  1856.8 11.7 convert_element_type.136
  1868.5 11.7 convert_element_type.139
  1880.1 9.5 convert_element_type.130
  (161 shorter events, 52.6 us)
Async XLA Ops:
  7.2 75.7 %copy-start = (bf16[512,2048]{1,0:T(8,128)(2,1)S(1)}, bf16[512,2048]{1,0:T(8,128)(2,1)}, u32[]{:S(2)}) copy-start(bf16[512,2048]{1,0:T(8,128)(2,1)} %param.23) | copy-start | bytes 6291460
  7.2 46.1 %copy-start.20 = (f32[2048]{0:T(1024)S(1)}, f32[2048]{0:T(1024)}, u32[]{:S(2)}) copy-start(f32[2048]{0:T(1024)} %param.19) | copy-start | bytes 24580
  7.2 46.1 %copy-start.29 = (f32[2048]{0:T(1024)S(1)}, f32[2048]{0:T(1024)}, u32[]{:S(2)}) copy-start(f32[2048]{0:T(1024)} %param.20) | copy-start | bytes 24580
  7.2 46.1 %copy-start.27 = (f32[3,512]{1,0:T(4,128)S(1)}, f32[3,512]{1,0:T(4,128)}, u32[]{:S(2)}) copy-start(f32[3,512]{1,0:T(4,128)} %param.22) | copy-start | bytes 18436
  7.2 39.6 %all-gather.5.cloned.1.call-start = ((), (), s32[]{:S(2)}) async-start(), calls=%async_computation.3 | async-start | bytes 5242880 | tf_op jit(solution)/shard_map/all_gather | solution.py:89
  8.0 75.0 %all-gather.11.cloned.1.call-start = ((), (), s32[]{:S(2)}) async-start(), calls=%async_computation.7 | async-start | bytes 5242880 | tf_op jit(solution)/shard_map/all_gather | solution.py:90
  8.7 157.2 %all-gather.9.cloned.1.call-start = ((), (), s32[]{:S(2)}) async-start(), calls=%async_computation.5 | async-start | bytes 5242880 | tf_op jit(solution)/shard_map/all_gather | solution.py:117
  11.8 53.2 %copy-start.13 = (f32[2,512,16]{1,2,0:T(8,128)}, f32[2,512,16]{1,2,0:T(8,128)S(1)}, u32[]{:S(2)}) copy-start(f32[2,512,16]{1,2,0:T(8,128)S(1)} %get-tuple-element.281) | copy-start | bytes 196612
  46.8 6.4 copy-start.3
  49.8 14.5 copy-start.18
  53.3 11.1 copy-start.16
  64.4 3.3 copy-start.8
  64.4 7.7 copy-start.12
  64.8 1.6 copy-start.7
  68.8 178.4 %all-gather.7.cloned.1.call-start = ((), (), s32[]{:S(2)}) async-start(), calls=%async_computation.4 | async-start | bytes 5242880 | tf_op jit(solution)/shard_map/all_gather | solution.py:118
  71.6 647.6 %reduce-scatter.6.cloned.1.call-start = ((), (), s32[]{:S(2)}) async-start(), calls=%async_computation.8 | async-start | bytes 10485760 | tf_op jit(solution)/shard_map/reduce_scatter | solution.py:221
  354.0 17.5 copy-start.1
  354.0 17.5 copy-start.2
  436.0 12.7 copy-start.5
  465.5 17.5 copy-start.1
  465.5 17.5 copy-start.2
  547.4 12.7 copy-start.5
  576.1 290.6 %reduce-scatter.8.cloned.1.call-start = ((), (), s32[]{:S(2)}) async-start(), calls=%async_computation.9 | async-start | bytes 10485760 | tf_op jit(solution)/shard_map/reduce_scatter | solution.py:227
  585.1 0.7 copy-start.17
  585.1 0.7 copy-start.19
  585.1 0.7 copy-start.21
  585.1 0.7 copy-start.30
  585.1 15.3 copy-start.11
  585.1 357.2 %reduce-scatter.4.cloned.1.call-start = ((), (), s32[]{:S(2)}) async-start(), calls=%async_computation.6 | async-start | bytes 10485760 | tf_op jit(solution)/shard_map/reduce_scatter | solution.py:155
  600.4 2.4 copy-start.28
  620.6 477.8 %all-reduce.6.cloned.1.call-start = ((), (), s32[]{:S(2)}) async-start(), calls=%async_computation.10 | async-start | bytes 16777216 | tf_op jit(solution)/shard_map/psum | solution.py:253
  640.1 13.5 copy-start.4
  640.1 25.5 %slice-start = ((s8[8388608]{0:T(1024)(128)(4,1)}), s8[4194304]{0:T(1024)(128)(4,1)S(1)}, s32[]{:S(2)}) async-start(s8[8388608]{0:T(1024)(128)(4,1)} %bitcast.267), calls=%async_computation.12 | async-start | bytes 8388608
  653.6 12.0 copy-start.26
  653.6 12.0 slice-start.1
  678.0 42.5 %copy-start.14 = (f32[2,512,16]{1,2,0:T(8,128)S(1)}, f32[2,512,16]{1,2,0:T(8,128)}, u32[]{:S(2)}) copy-start(f32[2,512,16]{1,2,0:T(8,128)} %copy-done.13) | copy-start | bytes 196612
  678.0 42.5 %copy-start.15 = (f32[2,512,16]{1,2,0:T(8,128)S(1)}, f32[2,512,16]{1,2,0:T(8,128)}, u32[]{:S(2)}) copy-start(f32[2,512,16]{1,2,0:T(8,128)} %get-tuple-element.279) | copy-start | bytes 196612
  868.4 13.5 copy-start.9
  881.9 975.0 %all-reduce.8.cloned.1.call-start = ((), (), s32[]{:S(2)}) async-start(), calls=%async_computation.11 | async-start | bytes 50331648 | tf_op jit(solution)/shard_map/psum | solution.py:274
  895.7 1.2 copy-start.6
  895.7 46.6 %copy-start.24 = (f32[512]{0:T(512)S(1)}, f32[512]{0:T(512)}, u32[]{:S(2)}) copy-start(f32[512]{0:T(512)} %param.28) | copy-start | bytes 6148
  895.7 46.6 %copy-start.25 = (f32[512]{0:T(512)S(1)}, f32[512]{0:T(512)}, u32[]{:S(2)}) copy-start(f32[512]{0:T(512)} %param.24) | copy-start | bytes 6148
  945.5 164.0 %copy-start.23 = (bf16[2048]{0:T(1024)(128)(2,1)S(1)}, bf16[2048]{0:T(1024)(128)(2,1)}, u32[]{:S(2)}) copy-start(bf16[2048]{0:T(1024)(128)(2,1)} %get-tuple-element.282) | copy-start | bytes 12292
  1150.6 741.7 %copy-start.22 = (f32[512]{0:T(512)}, f32[512]{0:T(512)S(1)}, u32[]{:S(2)}) copy-start(f32[512]{0:T(512)S(1)} %convert_element_type.134) | copy-start | bytes 6148
  1880.1 9.5 copy-start.10
Sparse Core Ops, SparseCore 0:
  9.6 37.1 all-gather.4
  48.4 34.4 all-gather.10
  85.1 80.7 all-gather.8
  167.9 79.2 all-gather.6
  576.2 142.9 reduce-scatter.5
  721.4 145.1 reduce-scatter.7
  869.8 72.4 reduce-scatter.3
  945.5 152.8 all-reduce.5
  1104.7 752.1 all-reduce.7
where the time goes:
time: 1910 us; the launch traced here: 1900 us
  waiting for transfers between devices  1270 us (66%)
  matrix products  366 us (19%)
  other arithmetic  166 us (9%)
  blocking collectives  39.8 us (2%)
  local copies, waits for them, and re-layouts  26.3 us (1%)
    psum x1, waiting for transfers between devices, local(): lax.psum(qkv_weight_grad.astype(jnp.bfloat16), ('dp', 'blk'))  701 us
    psum x1, waiting for transfers between devices, local(): gradient_complete = lax.psum(grad_normed, 'tensor')  153 us
    reduce_scatter x1, waiting for transfers between devices, local(): lax.psum_scatter(grad_values.reshape(row_count, length, local_width), 'bl...  138 us
    dot_general x4, matrix products, masked_scores(): jnp.einsum('qhd,khd->hqk', query_row, key_row, preferred_element_type=jnp...  82.6 us
    all_gather x1, waiting for transfers between devices, local(): lax.all_gather(values_here, 'blk', axis=1, tiled=True)  81.3 us
    all_gather x1, waiting for transfers between devices, local(): lax.all_gather(keys_here, 'blk', axis=1, tiled=True)  77.4 us
    convert_element_type x2, other arithmetic, backward_row(): grad_scores = (probs_exact * (grad_probs - delta_row)).astype(jnp.bfloat16)  54.8 us
    reduce_scatter x1, waiting for transfers between devices, local(): lax.psum_scatter(partial_sum, 'tensor', scatter_dimension=2, tiled=True)  42.7 us
  transfers between devices with their start and end apart: 9, of which 9 were waited for; matrix products, arithmetic and copies ran while one was open for 11% of the time, Pallas kernels for 0%

commit v1 on v0

v1 whole, which is shorter than its diff:
```python
import functools
import math

import jax
import jax.numpy as jnp
from jax import lax
from jax.experimental import pallas as pl
from jax.experimental.pallas import tpu as pltpu
from jax.sharding import PartitionSpec as P

HD = 64
ROT = 32
EPSILON = 1e-05
ROPE_LOG_BASE = math.log(10000.0)
NEGATIVE = -1e30
F32 = jnp.float32
BF = jnp.bfloat16
MESH = pl.DeviceIdType.MESH
dot32 = functools.partial(jnp.dot, preferred_element_type=F32)


def swap(value, axis, size, mask):
    return lax.ppermute(value, axis, [(i, i ^ mask) for i in range(size)])


def turn(source, cos_t, sin_t):
    half = ROT // 2
    front, back = source[:half], source[half:ROT]
    return jnp.concatenate(
        [front * cos_t - back * sin_t, back * cos_t + front * sin_t, source[ROT:]], axis=0
    )


def attention_kernel(
    nz, heads, tile, z_ref, pieces, grads, cos_ref, sin_ref, start_ref, out_ref,
    q_t, k_t, v_t, g_t, q_n, k_n, v_n, g_n, probs, dk_acc, dv_acc,
):
    z = z_ref[0]
    length = pieces[0].shape[0]
    width = heads * HD
    scale = HD**-0.5
    hs = range(heads)

    for m in range(nz):
        place = pl.ds(pl.multiple_of(jnp.bitwise_xor(z, m) * length, length), length)
        cos_t, sin_t = cos_ref[:, place], sin_ref[:, place]
        for h in hs:
            low = h * HD
            x = turn(pieces[m][:, low : low + HD].astype(F32).T, cos_t, sin_t) * scale
            q_t[h, :, place] = x.astype(BF)
            q_n[h, place, :] = x.T.astype(BF)
            low = width + h * HD
            x = turn(pieces[m][:, low : low + HD].astype(F32).T, cos_t, sin_t)
            k_t[h, :, place] = x.astype(BF)
            k_n[h, place, :] = x.T.astype(BF)
            low = 2 * width + h * HD
            x = pieces[m][:, low : low + HD]
            v_n[h, place, :] = x
            v_t[h, :, place] = x.astype(F32).T.astype(BF)
            x = grads[m][:, h * HD : h * HD + HD]
            g_n[h, place, :] = x
            g_t[h, :, place] = x.astype(F32).T.astype(BF)
    dk_acc[...] = jnp.zeros_like(dk_acc)
    dv_acc[...] = jnp.zeros_like(dv_acc)

    def one_tile(i, _):
        qs = pl.ds(pl.multiple_of(i * tile, tile), tile)
        start = start_ref[:, qs]
        queries = [q_t[h, :, qs] for h in hs]
        queries_n = [q_n[h, qs, :] for h in hs]
        cots = [g_t[h, :, qs] for h in hs]
        cots_n = [g_n[h, qs, :] for h in hs]
        key_at = lax.broadcasted_iota(jnp.int32, (tile, tile), 0)
        query_at = lax.broadcasted_iota(jnp.int32, (tile, tile), 1)

        def score(j, tops, diagonal):
            first = pl.multiple_of(j * tile, tile)
            allowed = key_at >= (start - first)
            if diagonal:
                allowed = allowed & (key_at <= query_at)
            result = []
            for h in hs:
                s = dot32(k_n[h, pl.ds(first, tile), :], queries[h])
                s = jnp.where(allowed, s, NEGATIVE)
                probs[h, pl.ds(first, tile), :] = s
                result.append(jnp.maximum(tops[h], jnp.max(s, axis=0, keepdims=True)))
            return tuple(result)

        tops = tuple(jnp.full((1, tile), NEGATIVE, F32) for _ in hs)
        tops = lax.fori_loop(0, i, lambda j, c: score(j, c, False), tops)
        tops = score(i, tops, True)

        def mix(j, carry):
            sums, mixed = carry
            ks = pl.ds(pl.multiple_of(j * tile, tile), tile)
            new_sums, new_mixed = [], []
            for h in hs:
                p = jnp.exp(probs[h, ks, :] - tops[h])
                probs[h, ks, :] = p
                new_sums.append(sums[h] + jnp.sum(p, axis=0, keepdims=True))
                new_mixed.append(mixed[h] + dot32(v_t[h, :, ks], p.astype(BF)))
            return tuple(new_sums), tuple(new_mixed)

        zeros = tuple(jnp.zeros((1, tile), F32) for _ in hs)
        wide_zeros = tuple(jnp.zeros((HD, tile), F32) for _ in hs)
        sums, mixed = lax.fori_loop(0, i + 1, mix, (zeros, wide_zeros))
        inverse = [1.0 / sums[h] for h in hs]
        mixed = [mixed[h] * inverse[h] for h in hs]
        delta = [jnp.sum(mixed[h] * cots[h].astype(F32), axis=0, keepdims=True) for h in hs]

        def back(j, carry):
            ks = pl.ds(pl.multiple_of(j * tile, tile), tile)
            result = []
            for h in hs:
                p = probs[h, ks, :] * inverse[h]
                dp = dot32(v_n[h, ks, :], cots[h])
                ds = (p * (dp - delta[h])).astype(BF)
                dv_acc[h, ks, :] += dot32(p.astype(BF), cots_n[h])
                dk_acc[h, ks, :] += dot32(ds, queries_n[h])
                result.append(carry[h] + dot32(k_t[h, :, ks], ds))
            return tuple(result)

        dq = lax.fori_loop(0, i + 1, back, wide_zeros)
        cos_t, sin_t = cos_ref[:, qs], sin_ref[:, qs]
        slot = jnp.bitwise_xor(i, z)
        for h in hs:
            low = h * HD
            out_ref[slot, :, low : low + HD] = turn(dq[h] * scale, cos_t, -sin_t).T.astype(BF)
            low = 3 * width + h * HD
            out_ref[slot, :, low : low + HD] = mixed[h].T.astype(BF)
        return 0

    lax.fori_loop(0, nz, one_tile, 0)
    for m in range(nz):
        place = pl.ds(pl.multiple_of(jnp.bitwise_xor(z, m) * length, length), length)
        cos_t, sin_t = cos_ref[:, place], sin_ref[:, place]
        for h in hs:
            low = width + h * HD
            x = turn(dk_acc[h, place, :].T, cos_t, -sin_t).T
            out_ref[m, :, low : low + HD] = x.astype(BF)
            low = 2 * width + h * HD
            out_ref[m, :, low : low + HD] = dv_acc[h, place, :].astype(BF)


def attention(z, pieces, grads, cos_t, sin_t, start):
    nz = len(pieces)
    length, width = grads[0].shape
    heads = width // HD
    total = nz * length

    def body(z_ref, *refs):
        attention_kernel(
            nz, heads, length, z_ref, refs[:nz], refs[nz : 2 * nz], *refs[2 * nz :]
        )

    vmem = pl.BlockSpec(memory_space=pltpu.VMEM)
    return pl.pallas_call(
        body,
        out_shape=jax.ShapeDtypeStruct((nz, length, 4 * width), BF),
        in_specs=[pl.BlockSpec(memory_space=pltpu.SMEM)] + [vmem] * (2 * nz + 3),
        out_specs=vmem,
        scratch_shapes=[pltpu.VMEM((heads, HD, total), BF)] * 4
        + [pltpu.VMEM((heads, total, HD), BF)] * 4
        + [pltpu.VMEM((heads, total, length), F32)]
        + [pltpu.VMEM((heads, total, HD), F32)] * 2,
        compiler_params=pltpu.CompilerParams(vmem_limit_bytes=56 << 20),
        cost_estimate=pl.CostEstimate(
            flops=heads * total * total * HD * 2 * 6 * 2,
            bytes_accessed=8 * total * width * 2,
            transcendentals=heads * total * total,
        ),
        name="attention",
    )(z, *pieces, *grads, cos_t, sin_t, start)


def add_rows(target, one, two):
    rows = target.shape[0]

    @pl.loop(0, rows, step=16)
    def _(r):
        at = pl.ds(pl.multiple_of(r, 16), 16)
        target[at] = (one[at].astype(F32) + two[at].astype(F32)).astype(BF)


def chain_kernel(chunks, count, *refs):
    own, refs = refs[:count], refs[count:]
    outs, refs = refs[:count], refs[count:]
    landed, refs = refs[:count], refs[count:]
    crossed, refs = refs[:count], refs[count:]
    stage, refs = refs[:count], refs[count:]
    sems, stage_sem, keep_sem = refs
    n = len(chunks)
    x, z = lax.axis_index("dp"), lax.axis_index("blk")
    at_end = (z == 0) | (z == 3)
    inner = jnp.where(z == 0, 1, 2)
    outer = jnp.where(z == 1, 0, 3)

    def send(kind, c, src, dst, device):
        return pltpu.make_async_remote_copy(
            src, dst, sems.at[2 * kind, c], sems.at[2 * kind + 1, c],
            device_id=device, device_id_type=MESH,
        )

    def rows(ref, c):
        a, first, size = chunks[c]
        return ref[a].at[pl.ds(first, size)]

    def final(c, half):
        a, first, size = chunks[c]
        return outs[a].at[half, pl.ds(first, size)]

    def go_in(c):
        return send(0, c, rows(own, c), rows(landed, c), {"blk": inner})

    def go_mid(c):
        return send(1, c, rows(landed, c), rows(crossed, c), {"blk": 3 - z})

    def go_out(c):
        return send(2, c, rows(crossed, c), final(c, x), {"blk": outer})

    def go_x_end(c):
        return send(3, c, final(c, x), final(c, x), {"dp": 1 - x})

    def go_x_mid(c):
        return send(3, c, rows(crossed, c), final(c, x), {"dp": 1 - x})

    def arrive_x(c):
        return send(3, c, final(c, 1 - x), final(c, 1 - x), {"dp": 1 - x})

    def arrive_out(c):
        return send(2, c, final(c, x), final(c, x), {"blk": inner})

    def load(c):
        a, first, size = chunks[c]
        return pltpu.make_async_copy(
            own[a].at[pl.ds(first, size)], stage[a].at[c % 3], stage_sem.at[c % 3]
        )

    def keep(c):
        return pltpu.make_async_copy(rows(crossed, c), final(c, x), keep_sem.at[c])

    barrier = pltpu.get_barrier_semaphore()
    pl.semaphore_signal(barrier, inc=1, device_id={"dp": 1 - x}, device_id_type=MESH)

    @pl.when(at_end)
    def _():
        pl.semaphore_signal(barrier, inc=1, device_id={"blk": inner}, device_id_type=MESH)
        pl.semaphore_wait(barrier, 2)
        lag = 4
        for c in range(n + lag):
            if c < n:
                if c >= 2:
                    go_in(c - 2).wait_send()
                go_in(c).start()
            if c >= lag:
                d = c - lag
                arrive_out(d).wait_recv()
                if d >= 2:
                    go_x_end(d - 2).wait_send()
                go_x_end(d).start()
        for c in range(n - 2, n):
            go_in(c).wait_send()
            go_x_end(c).wait_send()
        for c in range(n):
            arrive_x(c).wait_recv()

    @pl.when(jnp.logical_not(at_end))
    def _():
        pl.semaphore_signal(barrier, inc=1, device_id={"blk": outer}, device_id_type=MESH)
        pl.semaphore_signal(barrier, inc=1, device_id={"blk": 3 - z}, device_id_type=MESH)
        pl.semaphore_wait(barrier, 3)
        lag = 2
        for c in range(min(2, n)):
            load(c).start()
        for c in range(n + lag):
            if c < n:
                if c + 2 < n:
                    load(c + 2).start()
                load(c).wait()
                go_in(c).wait_recv()
                add_rows(rows(landed, c), rows(landed, c), stage[chunks[c][0]].at[c % 3])
                go_mid(c).start()
            if c >= lag:
                d = c - lag
                go_mid(d).wait_recv()
                add_rows(rows(crossed, d), rows(crossed, d), rows(landed, d))
                go_out(d).start()
                go_x_mid(d).start()
                keep(d).start()
        for c in range(n):
            go_mid(c).wait_send()
            go_out(c).wait_send()
            go_x_mid(c).wait_send()
            keep(c).wait()
        for c in range(n):
            arrive_x(c).wait_recv()


def chain(arrays, collective_id, chunk_bytes=1 << 19):
    chunks, stages = [], []
    for a, array in enumerate(arrays):
        rows, columns = array.shape
        size = min(rows, 1 << (chunk_bytes // (2 * columns)).bit_length() - 1)
        stages.append(pltpu.VMEM((3, size, columns), BF))
        chunks += [(a, first, size) for first in range(0, rows, size)]
    count = len(arrays)
    hbm = pl.BlockSpec(memory_space=pl.ANY)
    return pl.pallas_call(
        functools.partial(chain_kernel, chunks, count),
        out_shape=[jax.ShapeDtypeStruct((2,) + a.shape, BF) for a in arrays],
        in_specs=[hbm] * count,
        out_specs=[hbm] * count,
        scratch_shapes=[pltpu.VMEM(a.shape, BF) for a in arrays] * 2
        + stages
        + [
            pltpu.SemaphoreType.DMA((8, len(chunks))),
            pltpu.SemaphoreType.DMA((3,)),
            pltpu.SemaphoreType.DMA((len(chunks),)),
        ],
        compiler_params=pltpu.CompilerParams(
            collective_id=collective_id, has_side_effects=True, vmem_limit_bytes=56 << 20
        ),
        cost_estimate=pl.CostEstimate(
            flops=0, bytes_accessed=sum(a.size for a in arrays) * 60, transcendentals=0
        ),
        name="weight_sums",
    )(*arrays)


def place_blocks(blocks, order, count):
    width = blocks[0].shape[-1]
    out = jnp.zeros(blocks[0].shape[:-1] + (count * width,), blocks[0].dtype)
    for block, at in zip(blocks, order):
        out = lax.dynamic_update_slice_in_dim(out, block, at * width, out.ndim - 1)
    return out


def gather_all(part, nt):
    rows, tokens, width = part.shape
    x, t = lax.axis_index("dp"), lax.axis_index("tensor")
    if nt != 4:
        whole = lax.all_gather(part, "tensor", axis=2, tiled=True)
        return lax.all_gather(whole, "dp", axis=0, tiled=True)
    over_x = swap(part, "dp", 2, 1)
    over_y = swap(part, "tensor", 4, 2)
    half = tokens // 2
    corner = jnp.concatenate(
        [swap(over_y[:, :half], "dp", 2, 1), swap(over_x[:, half:], "tensor", 4, 2)], axis=1
    )
    mine = [(part, 0, 0), (over_x, 1, 0), (over_y, 0, 2), (corner, 1, 2)]
    blocks = mine + [(swap(b, "tensor", 4, 1), dx, dt + 1) for b, dx, dt in mine]
    out = jnp.zeros((2 * rows, tokens, nt * width), part.dtype)
    for block, dx, dt in blocks:
        at = (jnp.bitwise_xor(x, dx) * rows, 0, jnp.bitwise_xor(t, dt) * width)
        out = lax.dynamic_update_slice(out, block, at)
    return out


def scatter_sum(make, rows, tokens, width, nt):
    x, t = lax.axis_index("dp"), lax.axis_index("tensor")
    if nt != 4:
        whole = make(None).astype(BF)
        whole = lax.psum_scatter(whole, "dp", scatter_dimension=0, tiled=True)
        return lax.psum_scatter(whole, "tensor", scatter_dimension=2, tiled=True).astype(F32)
    core = t % 2
    other = swap(make(1 - core).astype(BF), "tensor", 4, 1)
    both = (make(core) + other.astype(F32)).astype(BF).reshape(2 * rows, tokens, 2, width)
    y = t // 2
    there = lax.dynamic_index_in_dim(both, 1 - y, 2, False)
    here = lax.dynamic_index_in_dim(both, y, 2, False)
    four = (here.astype(F32) + swap(there, "tensor", 4, 2).astype(F32)).astype(BF)
    away = lax.dynamic_slice_in_dim(four, (1 - x) * rows, rows, 0)
    near = lax.dynamic_slice_in_dim(four, x * rows, rows, 0)
    return near.astype(F32) + swap(away, "dp", 2, 1).astype(F32)


def core_columns(weight, nt, core):
    k, features = weight.shape
    cut = weight.reshape(k, 2, 2, features // 4)
    return lax.dynamic_index_in_dim(cut, core, 2, False).reshape(k, features // 2)


def butterfly(value, axes):
    for axis, size in axes:
        mask = 1
        while mask < size:
            value = value + swap(value, axis, size, mask)
            mask *= 2
    return value


def local(
    nx, nz, nt, block_input, segment_ids, layer_norm_gain, layer_norm_bias, qkv_weight, qkv_bias, out_weight, out_bias,
    up_weight, up_bias, down_weight, down_bias, grad_output,
):
    rows, tokens, width = block_input.shape
    all_rows = nx * rows
    features = nt * width
    many = all_rows * tokens
    x, z, t = lax.axis_index("dp"), lax.axis_index("blk"), lax.axis_index("tensor")
    att = qkv_weight.shape[2] // nx
    lanes = min(128, att)
    groups = att // lanes
    ff = up_weight.shape[1] // nx

    qkv_half = lax.dynamic_slice_in_dim(qkv_weight, x * att, att, 2)
    qkv_half_bias = lax.dynamic_slice_in_dim(qkv_bias, x * att, att, 1)
    out_half = lax.dynamic_slice_in_dim(out_weight, x * att, att, 0)
    up_half = lax.dynamic_slice_in_dim(up_weight, x * ff, ff, 1)
    up_half_bias = lax.dynamic_slice_in_dim(up_bias, x * ff, ff, 0)
    down_half = lax.dynamic_slice_in_dim(down_weight, x * ff, ff, 0)

    segments = lax.ppermute(segment_ids, "dp", [(0, 1), (1, 0)])
    segments = jnp.where(z // rows == x, segment_ids, segments)
    segments = lax.dynamic_slice_in_dim(segments, z % rows, 1, 0)
    length = segments.shape[1]
    places = jnp.arange(length, dtype=jnp.int32)[None]
    changed = jnp.concatenate(
        [jnp.ones((1, 1), dtype=bool), segments[:, 1:] != segments[:, :-1]], axis=1
    )
    start = lax.cummax(jnp.where(changed, places, 0), axis=1)
    half_rot = ROT // 2
    frequency = jnp.exp(jnp.arange(half_rot).astype(F32) * (-2.0 / ROT) * ROPE_LOG_BASE)
    angles = frequency[:, None] * (places - start).astype(F32)
    cos_t, sin_t = jnp.cos(angles), jnp.sin(angles)

    full_input = gather_all(block_input, nt)
    full_grad = gather_all(grad_output, nt)
    wide = full_input.astype(F32)
    mean = jnp.mean(wide, axis=-1, keepdims=True)
    centered = wide - mean
    variance = jnp.mean(centered * centered, axis=-1, keepdims=True)
    inverse_stddev = lax.rsqrt(variance + EPSILON)
    normed = (centered * inverse_stddev * layer_norm_gain + layer_norm_bias).astype(BF)
    normed = normed.reshape(many, features)
    cotangent = full_grad.reshape(many, features)

    z_at = z.astype(jnp.int32).reshape(1)
    results = []
    d_attended = dot32(cotangent, out_half.T).astype(BF).reshape(all_rows, tokens, att)
    for p in range(groups):
        w = qkv_half[:, :, p * lanes : (p + 1) * lanes].reshape(features, 3 * lanes)
        b = qkv_half_bias[:, p * lanes : (p + 1) * lanes].reshape(3 * lanes)
        qkv = (dot32(normed, w) + b).astype(BF).reshape(all_rows, tokens, 3 * lanes)
        d_att = d_attended[:, :, p * lanes : (p + 1) * lanes]

        def row(array, m):
            return lax.dynamic_index_in_dim(array, jnp.bitwise_xor(z, m), 0, False)

        pieces = [row(qkv, 0)] + [swap(row(qkv, m), "blk", nz, m) for m in range(1, nz)]
        grads = [row(d_att, 0)] + [swap(row(d_att, m), "blk", nz, m) for m in range(1, nz)]
        results.append(attention(z_at, pieces, grads, cos_t, sin_t, start))

    hidden = dot32(normed, up_half) + up_half_bias
    inner = math.sqrt(2.0 / math.pi) * (hidden + 0.044715 * hidden * hidden * hidden)
    tanh = jnp.tanh(inner)
    active = (0.5 * hidden * (1.0 + tanh)).astype(BF)
    slope = 0.5 * (1.0 + tanh) + 0.5 * hidden * (1.0 - tanh * tanh) * math.sqrt(2.0 / math.pi) * (
        1.0 + 3 * 0.044715 * hidden * hidden
    )
    d_hidden = (dot32(cotangent, down_half.T) * slope).astype(BF)
    down_part = dot32(active.T, cotangent).astype(BF)
    up_part = dot32(normed.T, d_hidden).astype(BF)
    up_bias_part = jnp.sum(d_hidden.astype(F32), axis=0)

    down_sum, up_sum = chain([down_part, up_part], 0)

    stacked = []
    for result in results:
        home = jnp.zeros((all_rows, tokens, 4 * lanes), BF)
        for m in range(nz):
            piece = result[m] if m == 0 else swap(result[m], "blk", nz, m)
            home = lax.dynamic_update_slice(home, piece[None], (jnp.bitwise_xor(z, m), 0, 0))
        stacked.append(home.reshape(many, 4 * lanes))
    d_qkv = [s[:, : 3 * lanes] for s in stacked]
    attended = [s[:, 3 * lanes :] for s in stacked]
    qkv_parts = [dot32(normed.T, d).astype(BF) for d in d_qkv]
    out_parts = [dot32(a.T, cotangent).astype(BF) for a in attended]
    qkv_bias_part = jnp.stack(
        [jnp.sum(d.astype(F32), axis=0).reshape(3, lanes) for d in d_qkv], axis=1
    ).reshape(3, att)

    def branch_share(core):
        def cols(weight):
            return weight if core is None else core_columns(weight, nt, core)

        total = dot32(active, cols(down_half))
        for p, a in enumerate(attended):
            total = total + dot32(a, cols(out_half[p * lanes : (p + 1) * lanes]))
        return total.reshape(all_rows, tokens, -1)

    def normed_share(core):
        def cols(weight):
            return weight if core is None else core_columns(weight, nt, core)

        total = dot32(d_hidden, cols(up_half.T))
        for p, d in enumerate(d_qkv):
            w = qkv_half[:, :, p * lanes : (p + 1) * lanes].reshape(features, 3 * lanes)
            total = total + dot32(d, cols(w.T))
        return total.reshape(all_rows, tokens, -1)

    branch = scatter_sum(branch_share, rows, tokens, width, nt)
    d_normed = scatter_sum(normed_share, rows, tokens, width, nt)

    sums = chain(out_parts + qkv_parts, 1)
    out_sums, qkv_sums = sums[:groups], sums[groups:]

    block_output = (block_input.astype(F32) + (branch + out_bias + down_bias)).astype(BF)

    gain = lax.dynamic_slice_in_dim(layer_norm_gain, t * width, width, 0)
    own_mean = lax.dynamic_slice_in_dim(mean, x * rows, rows, 0)
    own_inverse = lax.dynamic_slice_in_dim(inverse_stddev, x * rows, rows, 0)
    xhat = (block_input.astype(F32) - own_mean) * own_inverse
    scaled = d_normed * gain
    moments = jnp.stack([jnp.sum(scaled, axis=-1), jnp.sum(scaled * xhat, axis=-1)])
    moments = butterfly(moments, [("tensor", nt)]) / features
    first, second = moments[0][..., None], moments[1][..., None]
    input_grad = (
        grad_output.astype(F32) + own_inverse * (scaled - first - xhat * second)
    ).astype(BF)

    def spread(part, whole):
        shape = part.shape[:-1] + (whole,)
        at = (0,) * (part.ndim - 1) + (x * part.shape[-1],)
        return lax.dynamic_update_slice(jnp.zeros(shape, F32), part, at)

    small = [
        jnp.sum(d_normed * xhat, axis=(0, 1)),
        jnp.sum(d_normed, axis=(0, 1)),
        jnp.sum(grad_output.astype(F32), axis=(0, 1)),
        spread(up_bias_part, nx * ff),
        spread(qkv_bias_part, nx * att).reshape(-1),
    ]
    packed = butterfly(jnp.concatenate(small), [("dp", nx), ("blk", nz)])
    gain_grad, shift_grad, bias_grad = (packed[i * width : (i + 1) * width] for i in range(3))
    up_bias_grad = packed[3 * width : 3 * width + nx * ff]
    qkv_bias_grad = packed[3 * width + nx * ff :].reshape(3, nx * att)

    down_grad = down_sum.reshape(nx * ff, features).astype(F32)
    up_grad = jnp.swapaxes(up_sum, 0, 1).reshape(features, nx * ff).astype(F32)
    out_grad = jnp.stack(out_sums, axis=1).reshape(nx * att, features).astype(F32)
    qkv_grad = jnp.stack([s.reshape(nx, features, 3, lanes) for s in qkv_sums], axis=1)
    qkv_grad = jnp.transpose(qkv_grad, (2, 3, 0, 1, 4)).reshape(features, 3, nx * att).astype(F32)
    return (
        block_output, input_grad, gain_grad, shift_grad, qkv_grad, qkv_bias_grad, out_grad, bias_grad, up_grad,
        up_bias_grad, down_grad, bias_grad,
    )


def solution(mesh):
    in_specs = (
        P("dp", "blk", "tensor"), P("dp", None), P(), P(), P(None, None, "tensor"), P(None, "tensor"), P("tensor", None),
        P("tensor"), P(None, "tensor"), P("tensor"), P("tensor", None), P("tensor"), P("dp", "blk", "tensor"),
    )
    out_specs = (
        P("dp", "blk", "tensor"), P("dp", "blk", "tensor"), P("tensor"), P("tensor"), P(None, None, "tensor"),
        P(None, "tensor"), P("tensor", None), P("tensor"), P(None, "tensor"), P("tensor"), P("tensor", None), P("tensor"),
    )
    body = functools.partial(local, mesh.shape["dp"], mesh.shape["blk"], mesh.shape["tensor"])
    return jax.shard_map(body, mesh=mesh, in_specs=in_specs, out_specs=out_specs, check_vma=False)
```

time: 1910 us -> 1100 us (0.58)
  waiting for transfers between devices: 1270 us -> 152 us
  Pallas kernels: 0 us -> 430 us
  local copies, waits for them, and re-layouts: 26.3 us -> 228 us
  matrix products: 366 us -> 172 us
  other arithmetic: 166 us -> 67.7 us
  starting transfers between devices: 0.74 us -> 42.5 us
  blocking collectives: 39.8 us -> 0 us
    psum x2 -> x0, waiting for transfers between devices: 854 us -> none  [the longest x1 701 us: local(): lax.psum(qkv_weight_grad.astype(jnp.bfloat16), ('dp', 'blk'))]
    pallas_call x0 -> x4, Pallas kernels: none -> 430 us  [the longest x2 366 us: chain(): pl.pallas_call(functools.partial(chain_kernel, chunks, count), out_shape=...]
    reduce_scatter x3 -> x0, waiting for transfers between devices: 216 us -> none  [the longest x1 138 us: local(): lax.psum_scatter(grad_values.reshape(row_count, length, local_width), 'bl...]
    all_gather x4 -> x0, waiting for transfers between devices: 201 us -> none  [the longest x1 81.3 us: local(): lax.all_gather(values_here, 'blk', axis=1, tiled=True)]
    dot_general x26 -> x23, matrix products: 366 us -> 172 us  [the longest x1 19.5 us: local(): d_hidden = (dot32(cotangent, down_half.T) * slope).astype(BF)]
    ppermute x0 -> x46, waiting for transfers between devices: none -> 152 us  [the longest x45 152 us: swap(): return lax.ppermute(value, axis, [(i, i ^ mask) for i in range(size)])]
    unnamed x63 -> x165, local copies, waits for them, and re-layouts: 4.95 us -> 78.4 us
    convert_element_type x0 -> x5, local copies, waits for them, and re-layouts: none -> 46.9 us  [the longest x1 17.8 us: local(): up_grad = jnp.swapaxes(up_sum, 0, 1).reshape(features, nx * ff).astype(F32)]
  transfers between devices with their start and end apart: 9 -> 46, of which waited for: 9 -> 12; matrix products, arithmetic and copies ran while one was open for 11% -> 34% of each run, Pallas kernels for 0% -> 39%
where the time goes in v1:
time: 1100 us; the launch traced here: 1090 us
  Pallas kernels  430 us (39%)
  local copies, waits for them, and re-layouts  228 us (21%)
  matrix products  172 us (16%)
  waiting for transfers between devices  152 us (14%)
  other arithmetic  67.7 us (6%)
  starting transfers between devices  42.5 us (4%)
    pallas_call x2, Pallas kernels, chain(): pl.pallas_call(functools.partial(chain_kernel, chunks, count), out_shape=...  366 us
    ppermute x45, waiting for transfers between devices, swap(): return lax.ppermute(value, axis, [(i, i ^ mask) for i in range(size)])  152 us
    unnamed x165, local copies, waits for them, and re-layouts  78.4 us
    pallas_call x2, Pallas kernels, attention(): pl.pallas_call(body, out_shape=jax.ShapeDtypeStruct((nz, length, 4 * widt...  64.2 us
    ppermute x45, starting transfers between devices, swap(): return lax.ppermute(value, axis, [(i, i ^ mask) for i in range(size)])  41 us
  transfers between devices with their start and end apart: 46, of which 12 were waited for; matrix products, arithmetic and copies ran while one was open for 34% of the time, Pallas kernels for 39%

profile of v1, /device:TPU:0, one launch (start us, length us, event | category | flops | bytes accessed | tf_op | source)
XLA Modules:
  0.0 1093.6 jit_solution(16513839323751726357)
XLA Ops:
  20.3 4.8 constant_dynamic-slice_fusion.24
  25.1 6.4 copy.64
  49.1 7.6 constant_dynamic-slice_fusion.9
  56.7 7.7 constant_dynamic-slice_fusion.7
  91.8 19.4 %collective-permute-done.12 = bf16[2,512,512]{2,1,0:T(8,128)(2,1)S(1)} collective-permute-done((bf16[2,512,512]{2,1,0:T(8,128)(2,1)}, bf16[2,512,512]{2,1,0:T(8,128)(2,1)S(1)}, u32[]{:S(2)}, u32[]{:S(2)}) %collective-permute-start.12) | collective-permute-done | bytes 1048608 | tf_op jit(solution)/shard_map/ppermute | solution.py:23
  127.8 7.5 collective-permute-done.14
  154.9 5.8 convolution_convert_fusion.4
  164.2 13.1 %multiply_convert_fusion = (bf16[2048,1024]{1,0:T(8,128)(2,1)S(1)}, f32[2048,1024]{1,0:T(8,128)}) fusion(f32[1024]{0:T(1024)S(1)} %dynamic_slice.141, bf16[2048,2048]{1,0:T(8,128)(2,1)S(1)} %bitcast.212, bf16[2048,1024]{1,0:T(8,128)(2,1)S(1)} %copy-done.10), kind=kOutput, calls=%fused_computation.27 | convolution fusion | flops 8610906112 | bytes 25169920 | tf_op jit(solution)/shard_map/dot_general | solution.py:454
  177.3 19.5 %convert_reduce_fusion.1 = (f32[1024]{0:T(1024)S(1)}, bf16[2048,1024]{1,0:T(8,128)(2,1)}) fusion(f32[2048,1024]{1,0:T(8,128)} %get-tuple-element.107, f32[1024]{0:T(1024)S(1)} %dynamic_slice.141, bf16[2048,2048]{1,0:T(8,128)(2,1)} %bitcast.11, bf16[1024,2048]{1,0:T(8,128)(2,1)S(1)} %copy-done.6), kind=kOutput, calls=%fused_computation.20 | convolution fusion | flops 8636070912 | bytes 25174016 | tf_op jit(solution)/shard_map/dot_general | solution.py:461
  196.8 12.6 %convolution_convert_fusion.1.refs_1_ = bf16[2048,1024]{1,0:T(8,128)(2,1)} fusion(bf16[2048,2048]{1,0:T(8,128)(2,1)S(1)} %bitcast.213, bf16[2048,1024]{1,0:T(8,128)(2,1)} %get-tuple-element.109), kind=kOutput, calls=%fused_computation.33 | convolution fusion | flops 8592031744 | bytes 16777216 | tf_op jit(solution)/shard_map/dot_general | solution.py:463
  209.4 7.0 fusion.55
  216.5 4.8 add_convert_fusion.5
  231.9 6.9 fusion.56
  238.8 13.2 %convolution_convert_fusion.refs_0_ = bf16[1024,2048]{1,0:T(8,128)(2,1)} fusion(bf16[2048,1024]{1,0:T(8,128)(2,1)S(1)} %get-tuple-element.106, bf16[2048,2048]{1,0:T(8,128)(2,1)} %bitcast.11), kind=kOutput, calls=%fused_computation.32 | convolution fusion | flops 8592031744 | bytes 16777216 | tf_op jit(solution)/shard_map/dot_general | solution.py:462
  252.0 7.1 fusion.53
  259.1 6.9 fusion.54
  266.0 227.9 %weight_sums.3 = (bf16[2,1024,2048]{2,1,0:T(8,128)(2,1)}, bf16[2,2048,1024]{2,1,0:T(8,128)(2,1)}) custom-call(bf16[1024,2048]{1,0:T(8,128)(2,1)} %convolution_convert_fusion.refs_0_, bf16[2048,1024]{1,0:T(8,128)(2,1)} %convolution_convert_fusion.1.refs_1_), custom_call_target="tpu_custom_call" | custom-call | bytes 251658240 | tf_op jit(solution)/shard_map/weight_sums/pallas_call | solution.py:308
  493.8 11.7 %convert_bitcast_fusion = f32[2048,2,1024]{2,0,1:T(8,128)} fusion(bf16[2,2048,1024]{2,1,0:T(8,128)(2,1)} %get-tuple-element.22), kind=kLoop, calls=%fused_computation.8 | loop fusion | flops 4194304 | bytes 25165824 | tf_op jit(solution)/shard_map/convert_element_type | solution.py:540
  505.5 11.8 %bitcast_convert_fusion = f32[2048,2048]{1,0:T(8,128)} fusion(bf16[2,1024,2048]{2,1,0:T(8,128)(2,1)} %get-tuple-element.23), kind=kLoop, calls=%fused_computation.19 | loop fusion | flops 4194304 | bytes 25165824 | tf_op jit(solution)/shard_map/convert_element_type | solution.py:539
  517.3 8.0 add_convert_fusion.4
  526.7 17.8 %copy.59 = f32[2048,2,1024]{0,2,1:T(8,128)} copy(f32[2048,2,1024]{2,0,1:T(8,128)} %convert_bitcast_fusion) | data formatting | bytes 33554432 | tf_op jit(solution)/shard_map/convert_element_type | solution.py:540
  544.5 17.6 %copy.63 = f32[2048,2048]{1,0:T(8,128)} copy(f32[2048,2048]{0,1:T(8,128)} %bitcast.182) | data formatting | bytes 33554432
  571.5 32.1 %attention.2 = bf16[4,512,512]{2,1,0:T(8,128)(2,1)} custom-call(s32[1]{0:T(128)} %bitcast.3.z_ref, bf16[512,384]{1,0:T(8,128)(2,1)} %get-tuple-element.79.refs_0_, bf16[512,384]{1,0:T(8,128)(2,1)} %collective-permute-done.8.refs_1_, bf16[512,384]{1,0:T(8,128)(2,1)} %collective-permute-done.9.refs_2_, bf16[512,384]{1,0:T(8,128)(2,1)} %collective-permute-done.10.refs_3_, ...), custom_call_target="tpu_custom_call" | custom-call | flops 12884901888 | bytes 4194304 | tf_op jit(solution)/shard_map/attention/pallas_call | solution.py:157
  607.0 5.0 collective-permute-done.31.refs_7_
  614.0 32.1 %attention.3 = bf16[4,512,512]{2,1,0:T(8,128)(2,1)} custom-call(s32[1]{0:T(128)} %bitcast.3.z_ref, bf16[512,384]{1,0:T(8,128)(2,1)} %get-tuple-element.75.refs_0_, bf16[512,384]{1,0:T(8,128)(2,1)} %copy-done.57, bf16[512,384]{1,0:T(8,128)(2,1)} %copy-done.58, bf16[512,384]{1,0:T(8,128)(2,1)} %copy-done.59, bf16[512,128]{1,0:T(8,128)(2,1)} %get-tuple-element.92.refs_4_, ...), custom_call_target="tpu_custom_call" | custom-call | flops 12884901888 | bytes 4194304 | tf_op jit(solution)/shard_map/attention/pallas_call | solution.py:157
  653.0 9.8 collective-permute-done.32
  662.9 30.8 %collective-permute-done.33 = bf16[512,512]{1,0:T(8,128)(2,1)S(1)} collective-permute-done((bf16[512,512]{1,0:T(8,128)(2,1)S(1)}, bf16[512,512]{1,0:T(8,128)(2,1)S(1)}, u32[]{:S(2)}, u32[]{:S(2)}) %collective-permute-start.33) | collective-permute-done | bytes 524320 | tf_op jit(solution)/shard_map/ppermute | solution.py:23
  702.2 6.3 copy.52
  709.7 6.9 add_convert_fusion.3
  716.6 6.6 copy.45
  726.2 9.2 add_add_fusion
  735.4 8.7 copy.53
  745.7 8.4 add_add_fusion.1
  754.1 9.3 convolution_convert_fusion.3.refs_2_
  763.3 5.7 add_convert_fusion
  772.9 8.8 copy.46
  782.0 6.2 add_convert_fusion.2
  791.3 10.0 convolution_convert_fusion.2.refs_3_
  801.3 19.5 %collective-permute-done.39 = bf16[4,512,512]{1,2,0:T(8,128)(2,1)} collective-permute-done((bf16[4,512,512]{1,2,0:T(8,128)(2,1)}, bf16[4,512,512]{1,2,0:T(8,128)(2,1)}, u32[]{:S(2)}, u32[]{:S(2)}) %collective-permute-start.39) | collective-permute-done | bytes 2097184 | tf_op jit(solution)/shard_map/ppermute | solution.py:23
  826.0 5.6 convolution_convert_fusion.6.refs_0_
  831.6 33.3 %collective-permute-done.36 = bf16[4,512,512]{1,2,0:T(8,128)(2,1)} collective-permute-done((bf16[4,512,512]{1,2,0:T(8,128)(2,1)}, bf16[4,512,512]{1,2,0:T(8,128)(2,1)}, u32[]{:S(2)}, u32[]{:S(2)}) %collective-permute-start.36) | collective-permute-done | bytes 2097184 | tf_op jit(solution)/shard_map/ppermute | solution.py:23
  873.9 17.6 %collective-permute-done.37 = bf16[2,512,512]{1,2,0:T(8,128)(2,1)S(1)} collective-permute-done((bf16[2,512,512]{1,2,0:T(8,128)(2,1)S(1)}, bf16[2,512,512]{1,2,0:T(8,128)(2,1)S(1)}, u32[]{:S(2)}, u32[]{:S(2)}) %collective-permute-start.37) | collective-permute-done | bytes 1048608 | tf_op jit(solution)/shard_map/ppermute | solution.py:23
  895.5 5.7 convolution_convert_fusion.5.refs_1_
  901.1 137.8 %weight_sums.2 = (bf16[2,128,2048]{2,1,0:T(8,128)(2,1)}, bf16[2,128,2048]{2,1,0:T(8,128)(2,1)}, bf16[2,2048,384]{2,1,0:T(8,128)(2,1)}, bf16[2,2048,384]{2,1,0:T(8,128)(2,1)}) custom-call(bf16[128,2048]{1,0:T(8,128)(2,1)} %convolution_convert_fusion.6.refs_0_, bf16[128,2048]{1,0:T(8,128)(2,1)} %convolution_convert_fusion.5.refs_1_, ...), custom_call_target="tpu_custom_call" | custom-call | bytes 125829120 | tf_op jit(solution)/shard_map/weight_sums/pallas_call | solution.py:308
  1046.9 7.6 convert_bitcast_fusion.1
  1059.6 11.3 %copy.57 = f32[2048,3,2,2,128]{0,4,3,2,1:T(8,128)} copy(f32[2048,3,2,2,128]{0,4,1,2,3:T(8,128)} %convert_bitcast_fusion.1) | data formatting | bytes 25165824 | tf_op jit(solution)/shard_map/convert_element_type | solution.py:543
  1070.9 12.6 %copy.62 = f32[2048,3,512]{2,0,1:T(8,128)} copy(f32[2048,3,512]{0,2,1:T(8,128)} %bitcast.190) | data formatting | bytes 25165824
  1083.5 4.8 copy.58
  (353 shorter events, 195.2 us)
Async XLA Ops:
  0.6 89.9 %collective-permute-start = (bf16[2,512,512]{2,1,0:T(8,128)(2,1)}, bf16[2,512,512]{2,1,0:T(8,128)(2,1)}, u32[]{:S(2)}, u32[]{:S(2)}) collective-permute-start(bf16[2,512,512]{2,1,0:T(8,128)(2,1)} %param.13), channel_id=1, source_target_pairs={{0,16},{16,0},{1,17},{17,1},{2,18},{18,2},{3,19},{19,3},{4,20},{20... | collective-permute-start | bytes 3145736 | tf_op jit(solution)/shard_map/ppermute | solution.py:23
  3.6 84.5 %collective-permute-start.1 = (bf16[2,512,512]{2,1,0:T(8,128)(2,1)}, bf16[2,512,512]{2,1,0:T(8,128)(2,1)}, u32[]{:S(2)}, u32[]{:S(2)}) collective-permute-start(bf16[2,512,512]{2,1,0:T(8,128)(2,1)} %param.13), channel_id=1, source_target_pairs={{0,2},{1,3},{2,0},{3,1},{4,6},{5,7},{6,4},{7,5},{8,10},{9,11},{10,... | collective-permute-start | bytes 3145736 | tf_op jit(solution)/shard_map/ppermute | solution.py:23
  5.2 115.0 %collective-permute-start.4 = (bf16[2,512,512]{2,1,0:T(8,128)(2,1)}, bf16[2,512,512]{2,1,0:T(8,128)(2,1)}, u32[]{:S(2)}, u32[]{:S(2)}) collective-permute-start(bf16[2,512,512]{2,1,0:T(8,128)(2,1)} %param.13), channel_id=1, source_target_pairs={{0,1},{1,0},{2,3},{3,2},{4,5},{5,4},{6,7},{7,6},{8,9},{9,8},{10,11... | collective-permute-start | bytes 3145736 | tf_op jit(solution)/shard_map/ppermute | solution.py:23
  5.2 106.6 %collective-permute-start.11 = (bf16[2,512,512]{2,1,0:T(8,128)(2,1)}, bf16[2,512,512]{2,1,0:T(8,128)(2,1)}, u32[]{:S(2)}, u32[]{:S(2)}) collective-permute-start(bf16[2,512,512]{2,1,0:T(8,128)(2,1)} %param.25), channel_id=1, source_target_pairs={{0,16},{16,0},{1,17},{17,1},{2,18},{18,2},{3,19},{19,3},{4,20},{20... | collective-permute-start | bytes 3145736 | tf_op jit(solution)/shard_map/ppermute | solution.py:23
  5.7 80.3 %collective-permute-start.22 = (s32[2,2048]{1,0:T(2,128)}, s32[2,2048]{1,0:T(2,128)S(1)}, u32[]{:S(2)}, u32[]{:S(2)}) collective-permute-start(s32[2,2048]{1,0:T(2,128)} %param.14), channel_id=1, source_target_pairs={{0,16},{16,0},{1,17},{17,1},{2,18},{18,2},{3,19},{19,3},{4,20},{20... | collective-permute-start | bytes 49160 | tf_op jit(solution)/shard_map/ppermute | solution.py:413
  86.0 25.2 %collective-permute-start.12 = (bf16[2,512,512]{2,1,0:T(8,128)(2,1)}, bf16[2,512,512]{2,1,0:T(8,128)(2,1)S(1)}, u32[]{:S(2)}, u32[]{:S(2)}) collective-permute-start(bf16[2,512,512]{2,1,0:T(8,128)(2,1)} %param.25), channel_id=1, source_target_pairs={{0,2},{1,3},{2,0},{3,1},{4,6},{5,7},{6,4},{7,5},{8,10},{9,11},{10,... | collective-permute-start | bytes 3145736 | tf_op jit(solution)/shard_map/ppermute | solution.py:23
  88.1 38.0 %collective-permute-start.15 = (bf16[2,512,512]{2,1,0:T(8,128)(2,1)}, bf16[2,512,512]{2,1,0:T(8,128)(2,1)S(1)}, u32[]{:S(2)}, u32[]{:S(2)}) collective-permute-start(bf16[2,512,512]{2,1,0:T(8,128)(2,1)} %param.25), channel_id=1, source_target_pairs={{0,1},{1,0},{2,3},{3,2},{4,5},{5,4},{6,7},{7,6},{8,9},{9,8},{10,11... | collective-permute-start | bytes 3145736 | tf_op jit(solution)/shard_map/ppermute | solution.py:23
  90.5 32.4 %collective-permute-start.2 = (bf16[2,256,512]{2,1,0:T(8,128)(2,1)S(1)}, bf16[2,256,512]{2,1,0:T(8,128)(2,1)S(1)}, u32[]{:S(2)}, u32[]{:S(2)}) collective-permute-start(bf16[2,256,512]{2,1,0:T(8,128)(2,1)S(1)} %slice.157), channel_id=1, source_target_pairs={{0,16},{16,0},{1,17},{17,1},{2,18},{18,2},{3,19},{19,3},{4,20},{20... | collective-permute-start | bytes 1572872 | tf_op jit(solution)/shard_map/ppermute | solution.py:23
  111.2 14.9 %collective-permute-start.3 = (bf16[2,256,512]{2,1,0:T(8,128)(2,1)S(1)}, bf16[2,256,512]{2,1,0:T(8,128)(2,1)S(1)}, u32[]{:S(2)}, u32[]{:S(2)}) collective-permute-start(bf16[2,256,512]{2,1,0:T(8,128)(2,1)S(1)} %slice.158), channel_id=1, source_target_pairs={{0,2},{1,3},{2,0},{3,1},{4,6},{5,7},{6,4},{7,5},{8,10},{9,11},{10,... | collective-permute-start | bytes 1572872 | tf_op jit(solution)/shard_map/ppermute | solution.py:23
  111.7 16.0 %collective-permute-start.13 = (bf16[2,256,512]{2,1,0:T(8,128)(2,1)S(1)}, bf16[2,256,512]{2,1,0:T(8,128)(2,1)S(1)}, u32[]{:S(2)}, u32[]{:S(2)}) collective-permute-start(bf16[2,256,512]{2,1,0:T(8,128)(2,1)S(1)} %slice.159), channel_id=1, source_target_pairs={{0,16},{16,0},{1,17},{17,1},{2,18},{18,2},{3,19},{19,3},{4,20},{20... | collective-permute-start | bytes 1572872 | tf_op jit(solution)/shard_map/ppermute | solution.py:23
  120.1 15.2 %collective-permute-start.14 = (bf16[2,256,512]{2,1,0:T(8,128)(2,1)S(1)}, bf16[2,256,512]{2,1,0:T(8,128)(2,1)S(1)}, u32[]{:S(2)}, u32[]{:S(2)}) collective-permute-start(bf16[2,256,512]{2,1,0:T(8,128)(2,1)S(1)} %slice.160), channel_id=1, source_target_pairs={{0,2},{1,3},{2,0},{3,1},{4,6},{5,7},{6,4},{7,5},{8,10},{9,11},{10,... | collective-permute-start | bytes 1572872 | tf_op jit(solution)/shard_map/ppermute | solution.py:23
  122.9 16.9 %collective-permute-start.5 = (bf16[2,512,512]{2,1,0:T(8,128)(2,1)}, bf16[2,512,512]{2,1,0:T(8,128)(2,1)S(1)}, u32[]{:S(2)}, u32[]{:S(2)}) collective-permute-start(bf16[2,512,512]{2,1,0:T(8,128)(2,1)} %collective-permute-done), channel_id=1, source_target_pairs={{0,1},{1,0},{2,3},{3,2},{4,5},{5,4},{6,7},{7,6},{8,9},{9,8},{10,11... | collective-permute-start | bytes 3145736 | tf_op jit(solution)/shard_map/ppermute | solution.py:23
  126.1 15.3 %collective-permute-start.16 = (bf16[2,512,512]{2,1,0:T(8,128)(2,1)}, bf16[2,512,512]{2,1,0:T(8,128)(2,1)S(1)}, u32[]{:S(2)}, u32[]{:S(2)}) collective-permute-start(bf16[2,512,512]{2,1,0:T(8,128)(2,1)} %collective-permute-done.11), channel_id=1, source_target_pairs={{0,1},{1,0},{2,3},{3,2},{4,5},{5,4},{6,7},{7,6},{8,9},{9,8},{10,11... | collective-permute-start | bytes 3145736 | tf_op jit(solution)/shard_map/ppermute | solution.py:23
  126.1 16.4 %collective-permute-start.6 = (bf16[2,512,512]{2,1,0:T(8,128)(2,1)}, bf16[2,512,512]{2,1,0:T(8,128)(2,1)S(1)}, u32[]{:S(2)}, u32[]{:S(2)}) collective-permute-start(bf16[2,512,512]{2,1,0:T(8,128)(2,1)} %collective-permute-done.1), channel_id=1, source_target_pairs={{0,1},{1,0},{2,3},{3,2},{4,5},{5,4},{6,7},{7,6},{8,9},{9,8},{10,11... | collective-permute-start | bytes 3145736 | tf_op jit(solution)/shard_map/ppermute | solution.py:23
  127.7 15.8 %collective-permute-start.17 = (bf16[2,512,512]{2,1,0:T(8,128)(2,1)S(1)}, bf16[2,512,512]{2,1,0:T(8,128)(2,1)S(1)}, u32[]{:S(2)}, u32[]{:S(2)}) collective-permute-start(bf16[2,512,512]{2,1,0:T(8,128)(2,1)S(1)} %collective-permute-done.12), channel_id=1, source_target_pairs={{0,1},{1,0},{2,3},{3,2},{4,5},{5,4},{6,7},{7,6},{8,9},{9,8},{10,11... | collective-permute-start | bytes 3145736 | tf_op jit(solution)/shard_map/ppermute | solution.py:23
  135.3 9.3 collective-permute-start.7
  139.8 14.0 %collective-permute-start.18 = (bf16[2,512,512]{2,1,0:T(8,128)(2,1)S(1)}, bf16[2,512,512]{2,1,0:T(8,128)(2,1)S(1)}, u32[]{:S(2)}, u32[]{:S(2)}) collective-permute-start(bf16[2,512,512]{2,1,0:T(8,128)(2,1)S(1)} %constant_dynamic-update-slice_fusion.19), channel_id=1, source_target_pairs={{0,1},{1,0},{2,3},{3,2},{4,5},{5,4},{6,7},{7,6},{8,9},{9,8},{10,11... | collective-permute-start | bytes 3145736 | tf_op jit(solution)/shard_map/ppermute | solution.py:23
  164.2 52.3 %copy-start.14 = (bf16[4,512,2048]{2,1,0:T(8,128)(2,1)}, bf16[4,512,2048]{2,1,0:T(8,128)(2,1)S(1)}, u32[]{:S(2)}) copy-start(bf16[4,512,2048]{2,1,0:T(8,128)(2,1)S(1)} %fusion.5) | copy-start | bytes 25165828
  222.4 344.7 %collective-permute-start.8 = (bf16[512,384]{1,0:T(8,128)(2,1)}, bf16[512,384]{1,0:T(8,128)(2,1)}, u32[]{:S(2)}, u32[]{:S(2)}) collective-permute-start(bf16[512,384]{1,0:T(8,128)(2,1)} %get-tuple-element.78), channel_id=1, source_target_pairs={{0,4},{4,0},{8,12},{12,8},{1,5},{5,1},{9,13},{13,9},{2,6},{6,2},{1... | collective-permute-start | bytes 1179656 | tf_op jit(solution)/shard_map/ppermute | solution.py:23
  224.0 343.4 %collective-permute-start.9 = (bf16[512,384]{1,0:T(8,128)(2,1)S(1)}, bf16[512,384]{1,0:T(8,128)(2,1)}, u32[]{:S(2)}, u32[]{:S(2)}) collective-permute-start(bf16[512,384]{1,0:T(8,128)(2,1)S(1)} %get-tuple-element.77), channel_id=1, source_target_pairs={{0,8},{4,12},{8,0},{12,4},{1,9},{5,13},{9,1},{13,5},{2,10},{6,14},... | collective-permute-start | bytes 1179656 | tf_op jit(solution)/shard_map/ppermute | solution.py:23
  226.6 341.1 %collective-permute-start.10 = (bf16[512,384]{1,0:T(8,128)(2,1)S(1)}, bf16[512,384]{1,0:T(8,128)(2,1)}, u32[]{:S(2)}, u32[]{:S(2)}) collective-permute-start(bf16[512,384]{1,0:T(8,128)(2,1)S(1)} %get-tuple-element.76), channel_id=1, source_target_pairs={{0,12},{4,8},{8,4},{12,0},{1,13},{5,9},{9,5},{13,1},{2,14},{6,10},... | collective-permute-start | bytes 1179656 | tf_op jit(solution)/shard_map/ppermute | solution.py:23
  227.7 298.7 %collective-permute-start.19 = (bf16[512,128]{1,0:T(8,128)(2,1)S(1)}, bf16[512,128]{1,0:T(8,128)(2,1)S(1)}, u32[]{:S(2)}, u32[]{:S(2)}) collective-permute-start(bf16[512,128]{1,0:T(8,128)(2,1)S(1)} %get-tuple-element.95), channel_id=1, source_target_pairs={{0,4},{4,0},{8,12},{12,8},{1,5},{5,1},{9,13},{13,9},{2,6},{6,2},{1... | collective-permute-start | bytes 393224 | tf_op jit(solution)/shard_map/ppermute | solution.py:23
  228.4 334.6 %collective-permute-start.20 = (bf16[512,128]{1,0:T(8,128)(2,1)S(1)}, bf16[512,128]{1,0:T(8,128)(2,1)S(1)}, u32[]{:S(2)}, u32[]{:S(2)}) collective-permute-start(bf16[512,128]{1,0:T(8,128)(2,1)S(1)} %get-tuple-element.94), channel_id=1, source_target_pairs={{0,8},{4,12},{8,0},{12,4},{1,9},{5,13},{9,1},{13,5},{2,10},{6,14},... | collective-permute-start | bytes 393224 | tf_op jit(solution)/shard_map/ppermute | solution.py:23
  526.4 36.6 %collective-permute-start.21 = (bf16[512,128]{1,0:T(8,128)(2,1)S(1)}, bf16[512,128]{1,0:T(8,128)(2,1)S(1)}, u32[]{:S(2)}, u32[]{:S(2)}) collective-permute-start(bf16[512,128]{1,0:T(8,128)(2,1)S(1)} %get-tuple-element.93), channel_id=1, source_target_pairs={{0,12},{4,8},{8,4},{12,0},{1,13},{5,9},{9,5},{13,1},{2,14},{6,10},... | collective-permute-start | bytes 393224 | tf_op jit(solution)/shard_map/ppermute | solution.py:23
  563.0 49.7 %collective-permute-start.26 = (bf16[512,384]{1,0:T(8,128)(2,1)}, bf16[512,384]{1,0:T(8,128)(2,1)S(1)}, u32[]{:S(2)}, u32[]{:S(2)}) collective-permute-start(bf16[512,384]{1,0:T(8,128)(2,1)} %get-tuple-element.74), channel_id=1, source_target_pairs={{0,4},{4,0},{8,12},{12,8},{1,5},{5,1},{9,13},{13,9},{2,6},{6,2},{1... | collective-permute-start | bytes 1179656 | tf_op jit(solution)/shard_map/ppermute | solution.py:23
  563.0 50.1 %collective-permute-start.27 = (bf16[512,384]{1,0:T(8,128)(2,1)S(1)}, bf16[512,384]{1,0:T(8,128)(2,1)S(1)}, u32[]{:S(2)}, u32[]{:S(2)}) collective-permute-start(bf16[512,384]{1,0:T(8,128)(2,1)S(1)} %get-tuple-element.73), channel_id=1, source_target_pairs={{0,8},{4,12},{8,0},{12,4},{1,9},{5,13},{9,1},{13,5},{2,10},{6,14},... | collective-permute-start | bytes 1179656 | tf_op jit(solution)/shard_map/ppermute | solution.py:23
  567.1 46.0 %collective-permute-start.28 = (bf16[512,384]{1,0:T(8,128)(2,1)S(1)}, bf16[512,384]{1,0:T(8,128)(2,1)S(1)}, u32[]{:S(2)}, u32[]{:S(2)}) collective-permute-start(bf16[512,384]{1,0:T(8,128)(2,1)S(1)} %get-tuple-element.72), channel_id=1, source_target_pairs={{0,12},{4,8},{8,4},{12,0},{1,13},{5,9},{9,5},{13,1},{2,14},{6,10},... | collective-permute-start | bytes 1179656 | tf_op jit(solution)/shard_map/ppermute | solution.py:23
  567.4 36.2 %collective-permute-start.29 = (bf16[512,128]{1,0:T(8,128)(2,1)S(1)}, bf16[512,128]{1,0:T(8,128)(2,1)S(1)}, u32[]{:S(2)}, u32[]{:S(2)}) collective-permute-start(bf16[512,128]{1,0:T(8,128)(2,1)S(1)} %get-tuple-element.91), channel_id=1, source_target_pairs={{0,4},{4,0},{8,12},{12,8},{1,5},{5,1},{9,13},{13,9},{2,6},{6,2},{1... | collective-permute-start | bytes 393224 | tf_op jit(solution)/shard_map/ppermute | solution.py:23
  567.8 39.2 %collective-permute-start.30 = (bf16[512,128]{1,0:T(8,128)(2,1)S(1)}, bf16[512,128]{1,0:T(8,128)(2,1)S(1)}, u32[]{:S(2)}, u32[]{:S(2)}) collective-permute-start(bf16[512,128]{1,0:T(8,128)(2,1)S(1)} %get-tuple-element.90), channel_id=1, source_target_pairs={{0,8},{4,12},{8,0},{12,4},{1,9},{5,13},{9,1},{13,5},{2,10},{6,14},... | collective-permute-start | bytes 393224 | tf_op jit(solution)/shard_map/ppermute | solution.py:23
  603.6 8.4 collective-permute-start.31
  607.0 45.1 %collective-permute-start.23 = (bf16[512,512]{1,0:T(8,128)(2,1)S(1)}, bf16[512,512]{1,0:T(8,128)(2,1)S(1)}, u32[]{:S(2)}, u32[]{:S(2)}) collective-permute-start(bf16[512,512]{1,0:T(8,128)(2,1)S(1)} %get-tuple-element.66), channel_id=1, source_target_pairs={{0,4},{4,0},{8,12},{12,8},{1,5},{5,1},{9,13},{13,9},{2,6},{6,2},{1... | collective-permute-start | bytes 1572872 | tf_op jit(solution)/shard_map/ppermute | solution.py:23
  612.0 41.0 %collective-permute-start.24 = (bf16[512,512]{1,0:T(8,128)(2,1)S(1)}, bf16[512,512]{1,0:T(8,128)(2,1)S(1)}, u32[]{:S(2)}, u32[]{:S(2)}) collective-permute-start(bf16[512,512]{1,0:T(8,128)(2,1)S(1)} %get-tuple-element.65), channel_id=1, source_target_pairs={{0,8},{4,12},{8,0},{12,4},{1,9},{5,13},{9,1},{13,5},{2,10},{6,14},... | collective-permute-start | bytes 1572872 | tf_op jit(solution)/shard_map/ppermute | solution.py:23
  612.7 40.3 %collective-permute-start.25 = (bf16[512,512]{1,0:T(8,128)(2,1)S(1)}, bf16[512,512]{1,0:T(8,128)(2,1)S(1)}, u32[]{:S(2)}, u32[]{:S(2)}) collective-permute-start(bf16[512,512]{1,0:T(8,128)(2,1)S(1)} %get-tuple-element.64), channel_id=1, source_target_pairs={{0,12},{4,8},{8,4},{12,0},{1,13},{5,9},{9,5},{13,1},{2,14},{6,10},... | collective-permute-start | bytes 1572872 | tf_op jit(solution)/shard_map/ppermute | solution.py:23
  646.3 47.4 %copy-start.27 = (bf16[384,2,1,512]{0,3,1,2:T(8,128)(2,1)S(1)}, bf16[384,2,1,512]{0,3,1,2:T(8,128)(2,1)}, u32[]{:S(2)}) copy-start(bf16[384,2,1,512]{0,3,1,2:T(8,128)(2,1)} %copy.71) | copy-start | bytes 2359300
  648.1 14.7 %collective-permute-start.32 = (bf16[512,512]{1,0:T(8,128)(2,1)S(1)}, bf16[512,512]{1,0:T(8,128)(2,1)S(1)}, u32[]{:S(2)}, u32[]{:S(2)}) collective-permute-start(bf16[512,512]{1,0:T(8,128)(2,1)S(1)} %get-tuple-element.60), channel_id=1, source_target_pairs={{0,4},{4,0},{8,12},{12,8},{1,5},{5,1},{9,13},{13,9},{2,6},{6,2},{1... | collective-permute-start | bytes 1572872 | tf_op jit(solution)/shard_map/ppermute | solution.py:23
  650.4 43.2 %collective-permute-start.33 = (bf16[512,512]{1,0:T(8,128)(2,1)S(1)}, bf16[512,512]{1,0:T(8,128)(2,1)S(1)}, u32[]{:S(2)}, u32[]{:S(2)}) collective-permute-start(bf16[512,512]{1,0:T(8,128)(2,1)S(1)} %get-tuple-element.59), channel_id=1, source_target_pairs={{0,8},{4,12},{8,0},{12,4},{1,9},{5,13},{9,1},{13,5},{2,10},{6,14},... | collective-permute-start | bytes 1572872 | tf_op jit(solution)/shard_map/ppermute | solution.py:23
  652.1 44.1 %collective-permute-start.34 = (bf16[512,512]{1,0:T(8,128)(2,1)S(1)}, bf16[512,512]{1,0:T(8,128)(2,1)S(1)}, u32[]{:S(2)}, u32[]{:S(2)}) collective-permute-start(bf16[512,512]{1,0:T(8,128)(2,1)S(1)} %get-tuple-element.58), channel_id=1, source_target_pairs={{0,12},{4,8},{8,4},{12,0},{1,13},{5,9},{9,5},{13,1},{2,14},{6,10},... | collective-permute-start | bytes 1572872 | tf_op jit(solution)/shard_map/ppermute | solution.py:23
  708.4 54.9 %collective-permute-start.38 = (bf16[4,512,1024]{1,2,0:T(8,128)(2,1)}, bf16[4,512,1024]{1,2,0:T(8,128)(2,1)}, u32[]{:S(2)}, u32[]{:S(2)}) collective-permute-start(bf16[4,512,1024]{1,2,0:T(8,128)(2,1)} %copy.52), channel_id=1, source_target_pairs={{0,1},{1,0},{2,3},{3,2},{4,5},{5,4},{6,7},{7,6},{8,9},{9,8},{10,11... | collective-permute-start | bytes 12582920 | tf_op jit(solution)/shard_map/ppermute | solution.py:23
  723.2 58.8 %collective-permute-start.35 = (bf16[4,512,1024]{1,2,0:T(8,128)(2,1)}, bf16[4,512,1024]{1,2,0:T(8,128)(2,1)}, u32[]{:S(2)}, u32[]{:S(2)}) collective-permute-start(bf16[4,512,1024]{1,2,0:T(8,128)(2,1)} %copy.45), channel_id=1, source_target_pairs={{0,1},{1,0},{2,3},{3,2},{4,5},{5,4},{6,7},{7,6},{8,9},{9,8},{10,11... | collective-permute-start | bytes 12582920 | tf_op jit(solution)/shard_map/ppermute | solution.py:23
  772.0 48.8 %collective-permute-start.39 = (bf16[4,512,512]{1,2,0:T(8,128)(2,1)}, bf16[4,512,512]{1,2,0:T(8,128)(2,1)}, u32[]{:S(2)}, u32[]{:S(2)}) collective-permute-start(bf16[4,512,512]{1,2,0:T(8,128)(2,1)} %dynamic-slice_bitcast_fusion), channel_id=1, source_target_pairs={{0,2},{1,3},{2,0},{3,1},{4,6},{5,7},{6,4},{7,5},{8,10},{9,11},{10,... | collective-permute-start | bytes 6291464 | tf_op jit(solution)/shard_map/ppermute | solution.py:23
  789.7 75.2 %collective-permute-start.36 = (bf16[4,512,512]{1,2,0:T(8,128)(2,1)}, bf16[4,512,512]{1,2,0:T(8,128)(2,1)}, u32[]{:S(2)}, u32[]{:S(2)}) collective-permute-start(bf16[4,512,512]{1,2,0:T(8,128)(2,1)} %dynamic-slice_bitcast_fusion.1), channel_id=1, source_target_pairs={{0,2},{1,3},{2,0},{3,1},{4,6},{5,7},{6,4},{7,5},{8,10},{9,11},{10,... | collective-permute-start | bytes 6291464 | tf_op jit(solution)/shard_map/ppermute | solution.py:23
  825.4 42.4 %collective-permute-start.40 = (bf16[2,512,512]{1,2,0:T(8,128)(2,1)}, bf16[2,512,512]{1,2,0:T(8,128)(2,1)S(1)}, u32[]{:S(2)}, u32[]{:S(2)}) collective-permute-start(bf16[2,512,512]{1,2,0:T(8,128)(2,1)} %constant_dynamic-slice_fusion.6), channel_id=1, source_target_pairs={{0,16},{16,0},{1,17},{17,1},{2,18},{18,2},{3,19},{19,3},{4,20},{20... | collective-permute-start | bytes 3145736 | tf_op jit(solution)/shard_map/ppermute | solution.py:23
  867.2 24.3 %collective-permute-start.37 = (bf16[2,512,512]{1,2,0:T(8,128)(2,1)S(1)}, bf16[2,512,512]{1,2,0:T(8,128)(2,1)S(1)}, u32[]{:S(2)}, u32[]{:S(2)}) collective-permute-start(bf16[2,512,512]{1,2,0:T(8,128)(2,1)S(1)} %constant_dynamic-slice_fusion.14), channel_id=1, source_target_pairs={{0,16},{16,0},{1,17},{17,1},{2,18},{18,2},{3,19},{19,3},{4,20},{20... | collective-permute-start | bytes 3145736 | tf_op jit(solution)/shard_map/ppermute | solution.py:23
  868.9 1.2 collective-permute-start.41
  870.1 3.7 collective-permute-start.42
  894.9 151.9 %collective-permute-start.43 = (f32[5120]{0:T(1024)S(1)}, f32[5120]{0:T(1024)S(1)}, u32[]{:S(2)}, u32[]{:S(2)}) collective-permute-start(f32[5120]{0:T(1024)S(1)} %constant_dynamic-update-slice_fusion.22), channel_id=1, source_target_pairs={{0,16},{16,0},{1,17},{17,1},{2,18},{18,2},{3,19},{19,3},{4,20},{20... | collective-permute-start | bytes 61448 | tf_op jit(solution)/shard_map/ppermute | solution.py:23
  1046.8 7.7 collective-permute-start.44
  1054.5 36.5 %collective-permute-start.45 = (f32[5120]{0:T(1024)S(1)}, f32[5120]{0:T(1024)S(1)}, u32[]{:S(2)}, u32[]{:S(2)}) collective-permute-start(f32[5120]{0:T(1024)S(1)} %add.352), channel_id=1, source_target_pairs={{0,8},{4,12},{8,0},{12,4},{1,9},{5,13},{9,1},{13,5},{2,10},{6,14},... | collective-permute-start | bytes 61448 | tf_op jit(solution)/shard_map/ppermute | solution.py:23
  (69 other events, 692.2 us)

commit v2 on v1

v2 whole, which is shorter than its diff:
```python
import functools
import math

import jax
import jax.numpy as jnp
from jax import lax
from jax.experimental import pallas as pl
from jax.experimental.pallas import tpu as pltpu
from jax.sharding import PartitionSpec as P

HD = 64
ROT = 32
EPSILON = 1e-05
ROPE_LOG_BASE = math.log(10000.0)
NEGATIVE = -1e30
F32 = jnp.float32
BF = jnp.bfloat16
MESH = pl.DeviceIdType.MESH
dot32 = functools.partial(jnp.dot, preferred_element_type=F32)


def swap(value, axis, size, mask):
    return lax.ppermute(value, axis, [(i, i ^ mask) for i in range(size)])


def flip(index, mask):
    if mask == 0:
        return index
    if mask == 1:
        return index + 1 - 2 * (index % 2)
    if mask == 2:
        return (index + 2) % 4
    return 3 - index


def front_kernel(
    gather, split, rows, tokens, x_own, g_own, gain_ref, shift_ref, wq_ref, bq_ref, wo_ref, wu_ref, bu_ref, wd_ref,
    normed_o, g_o, land_o, stats_o, down_o, up_o, branch_o, dnorm_o, ubias_o,
    xin, gin, vq, vo, vu, vd, pay, act, slope, stage, gather_sems, land_sems, load_sems, keep_sems, stage_sems,
):
    x, z, t = lax.axis_index("dp"), lax.axis_index("blk"), lax.axis_index("tensor")
    many, features = xin.shape
    half = rows * tokens
    width = features // 4
    att = vq.shape[2]
    ff = vu.shape[1]
    nz = pay.shape[0]
    wide = min(512, ff)

    def remote(src, dst, sems, device):
        return pltpu.make_async_remote_copy(
            src, dst, sems[0], sems[1], device_id=device, device_id_type=MESH
        )

    peers = {"x": {"dp": 1 - x}, "y": {"tensor": flip(t, 2)}, "c": {"tensor": flip(t, 1)}}
    barrier = pltpu.get_barrier_semaphore()
    greet = [{"blk": flip(z, m)} for m in range(1, nz)] + (list(peers.values()) if gather else [])
    for device in greet:
        pl.semaphore_signal(barrier, inc=1, device_id=device, device_id_type=MESH)

    loads = [
        pltpu.make_async_copy(
            wq_ref.at[:, :, pl.ds(pl.multiple_of(x * att, 128), att)] if split else wq_ref, vq, load_sems.at[0]
        ),
        pltpu.make_async_copy(
            wu_ref.at[:, pl.ds(pl.multiple_of(x * ff, 128), ff)] if split else wu_ref, vu, load_sems.at[1]
        ),
        pltpu.make_async_copy(wd_ref.at[pl.ds(x * ff, ff)] if split else wd_ref, vd, load_sems.at[2]),
        pltpu.make_async_copy(wo_ref.at[pl.ds(x * att, att)] if split else wo_ref, vo, load_sems.at[3]),
    ]
    if not gather:
        both = [
            pltpu.make_async_copy(x_own, xin, load_sems.at[4]),
            pltpu.make_async_copy(g_own, gin, load_sems.at[5]),
        ]
    else:
        both = [
            pltpu.make_async_copy(
                own,
                buf.at[pl.ds(x * half, half), pl.ds(pl.multiple_of(t * width, 128), width)],
                load_sems.at[4 + i],
            )
            for i, (own, buf) in enumerate([(x_own, xin), (g_own, gin)])
        ]
    both[0].start()
    both[1].start()
    pl.semaphore_wait(barrier, len(greet))

    class Gather:
        def __init__(self, which, own, buf):
            self.which, self.own, self.buf, self.names = which, own, buf, []

        def at(self, dx, dt, r):
            return self.buf.at[
                pl.ds(pl.multiple_of((1 - x if dx else x) * half + r * tokens, tokens), tokens),
                pl.ds(pl.multiple_of(flip(t, dt) * width, 128), width),
            ]

        plan = {
            "x": (0, 0, "x", 1, 0), "y": (0, 0, "y", 0, 2), "c": (0, 0, "c", 0, 1),
            "ex": (1, 0, "c", 1, 1), "ey": (0, 2, "c", 0, 3), "ed": (1, 2, "c", 1, 3),
        }

        def sems(self, kind, r):
            k = 2 * ("x", "y", "c", "d", "ex", "ey", "ed").index(kind) + r
            return gather_sems.at[self.which, 0, k], gather_sems.at[self.which, 1, k]

        def copy(self, kind, r):
            if kind == "d":
                dx, dt, to = (1, 0, "y") if r == 0 else (0, 2, "x")
            else:
                dx, dt, to = self.plan[kind][:3]
            src = dst = self.at(dx, dt, r)
            if kind in "xyc":
                src = self.own.at[pl.ds(r * tokens, tokens)]
            return remote(src, dst, self.sems(kind, r), peers[to])

        def start(self, kind, r):
            self.names.append((kind, r))
            self.copy(kind, r).start()

        def wait(self, kind, r):
            if kind == "d":
                dx, dt, to = 1, 2, "y"
            else:
                to, dx, dt = self.plan[kind][2:]
            ref = self.at(dx, dt, r)
            remote(ref, ref, self.sems(kind, r), peers[to]).wait_recv()

        def first(self):
            for kind, r in (("x", 0), ("y", 1), ("x", 1), ("y", 0), ("c", 0), ("c", 1)):
                self.start(kind, r)

        def second(self):
            self.wait("x", 0)
            self.start("d", 0)
            self.start("ex", 0)
            self.wait("y", 1)
            self.start("d", 1)
            self.start("ey", 1)

        def third(self):
            self.wait("x", 1)
            self.start("ex", 1)
            self.wait("y", 0)
            self.start("ey", 0)

        def fourth(self):
            self.wait("d", 0)
            self.start("ed", 0)
            self.wait("d", 1)
            self.start("ed", 1)

        def last(self):
            for kind in ("c", "ex", "ey", "ed"):
                for r in range(2):
                    self.wait(kind, r)

        def drain(self):
            for kind, r in self.names:
                self.copy(kind, r).wait_send()

    ins, cots = Gather(0, x_own, xin), Gather(1, g_own, gin)
    if gather:
        ins.first()
    for load in loads:
        load.start()
    if gather:
        ins.second()
        ins.third()
        cots.first()
        ins.fourth()
    both[0].wait()
    if gather:
        ins.last()
        ins.drain()

    @pl.loop(0, many // 128)
    def _(i):
        at = pl.ds(pl.multiple_of(i * 128, 128), 128)
        v = xin[at, :].astype(F32)
        mean = jnp.sum(v, axis=-1, keepdims=True) * (1.0 / features)
        v = v - mean
        inverse = lax.rsqrt(jnp.sum(v * v, axis=-1, keepdims=True) * (1.0 / features) + EPSILON)
        xin[at, :] = (v * inverse * gain_ref[...] + shift_ref[...]).astype(BF)
        lane = lax.broadcasted_iota(jnp.int32, (128, 128), 1)
        stats_o[at, :] = jnp.where(lane < 64, mean, inverse)

    keep_normed = pltpu.make_async_copy(xin, normed_o, keep_sems.at[0])
    keep_normed.start()
    if gather:
        cots.second()

    def place(position):
        return pl.ds(pl.multiple_of(position * tokens, tokens), tokens)

    def send(kind, m):
        parts = pl.ds(0, 3) if kind == 0 else pl.ds(3, 1)
        src, dst = pay.at[flip(z, m), parts], land_o.at[parts, place(z)]
        if m == 0:
            return pltpu.make_async_copy(src, dst, keep_sems.at[2 + kind])
        sems = land_sems.at[0, kind, m], land_sems.at[1, kind, m]
        return remote(src, dst, sems, {"blk": flip(z, m)})

    def landed(kind, m):
        parts = pl.ds(0, 3) if kind == 0 else pl.ds(3, 1)
        ref = land_o.at[parts, place(flip(z, m))]
        sems = land_sems.at[0, kind, m], land_sems.at[1, kind, m]
        return remote(ref, ref, sems, {"blk": flip(z, m)})

    order = [m for m in (2, 3, 1, 0) if m < nz]
    loads[0].wait()
    for m in order:
        row = flip(z, m)

        @pl.loop(0, 3)
        def _(part):
            value = dot32(xin[place(row), :], vq[part]) + bq_ref[part]
            pay[row, part] = value.astype(BF)

        send(0, m).start()
    if gather:
        cots.third()

    loads[1].wait()

    @pl.loop(0, many // tokens)
    def _(i):
        at = place(i)

        @pl.loop(0, ff // wide)
        def _(j):
            columns = pl.ds(pl.multiple_of(j * wide, wide), wide)
            h = dot32(xin[at, :], vu[:, columns]) + bu_ref[:, columns]
            c = math.sqrt(2.0 / math.pi)
            square = h * h
            tanh = jnp.tanh(c * h * (1.0 + 0.044715 * square))
            one = 0.5 * (1.0 + tanh)
            act[at, columns] = (h * one).astype(BF)
            d = one + 0.5 * h * (1.0 - tanh * tanh) * (c * (1.0 + 3 * 0.044715 * square))
            slope[at, columns] = d.astype(BF)

    if gather:
        cots.fourth()
    both[1].wait()
    if gather:
        cots.last()
    keep_g = pltpu.make_async_copy(gin, g_o, keep_sems.at[1])
    keep_g.start()

    loads[3].wait()
    nt_dims = (((1,), (1,)), ((), ()))
    tn_dims = (((0,), (0,)), ((), ()))
    general = functools.partial(lax.dot_general, preferred_element_type=F32)
    for m in order:
        row = flip(z, m)
        pay[row, 3] = general(gin[place(row), :], vo[...], nt_dims).astype(BF)
        send(1, m).start()

    loads[2].wait()
    ubias_o[...] = jnp.zeros_like(ubias_o)

    @pl.loop(0, many // tokens)
    def _(i):
        at = place(i)

        @pl.loop(0, ff // wide)
        def _(j):
            columns = pl.ds(pl.multiple_of(j * wide, wide), wide)
            d = general(gin[at, :], vd[columns, :], nt_dims) * slope[at, columns].astype(F32)
            d = d.astype(BF)
            slope[at, columns] = d
            ubias_o[0:1, columns] += jnp.sum(d.astype(F32), axis=0, keepdims=True)

    def through(steps, rows_of, columns_of, make, out):
        def copy(i):
            return pltpu.make_async_copy(
                stage.at[i % 2, pl.ds(0, rows_of), pl.ds(0, columns_of)],
                out.at[pl.ds(pl.multiple_of(i * rows_of, rows_of), rows_of)],
                stage_sems.at[i % 2],
            )

        @pl.loop(0, steps)
        def _(i):
            @pl.when(i >= 2)
            def _():
                copy(i - 2).wait()

            make(i, stage.at[i % 2, pl.ds(0, rows_of), pl.ds(0, columns_of)])
            copy(i).start()

        for i in range(max(0, steps - 2), steps):
            copy(i).wait()

    def down_tile(i, target):
        f = pl.ds(pl.multiple_of(i * 256, 256), 256)
        for j in range(0, features, 1024):
            target[:, j : j + 1024] = general(act[:, f], gin[:, j : j + 1024], tn_dims).astype(BF)

    through(ff // 256, 256, features, down_tile, down_o)

    def up_tile(i, target):
        f = pl.ds(pl.multiple_of(i * 256, 256), 256)
        target[...] = general(xin[:, f], slope[...], tn_dims).astype(BF)

    through(features // 256, 256, ff, up_tile, up_o)

    def branch_tile(i, target):
        @pl.loop(0, features // 512)
        def _(j):
            columns = pl.ds(pl.multiple_of(j * 512, 512), 512)
            target[:, columns] = dot32(act[place(i), :], vd[:, columns]).astype(BF)

    through(many // tokens, tokens, features, branch_tile, branch_o)

    def dnorm_tile(i, target):
        @pl.loop(0, features // 512)
        def _(j):
            columns = pl.ds(pl.multiple_of(j * 512, 512), 512)
            target[:, columns] = general(slope[place(i), :], vu[columns, :], nt_dims).astype(BF)

    through(many // tokens, tokens, features, dnorm_tile, dnorm_o)

    keep_normed.wait()
    keep_g.wait()
    for kind in range(2):
        for m in range(nz):
            if m == 0:
                send(kind, 0).wait()
            else:
                send(kind, m).wait_send()
                landed(kind, m).wait_recv()
    if gather:
        cots.drain()


def front(gather, split, rows, tokens, nz, many, features, att, ff, operands):
    hbm = pl.BlockSpec(memory_space=pl.ANY)
    vmem = pl.BlockSpec(memory_space=pltpu.VMEM)
    return pl.pallas_call(
        functools.partial(front_kernel, gather, split, rows, tokens),
        out_shape=[
            jax.ShapeDtypeStruct((many, features), BF),
            jax.ShapeDtypeStruct((many, features), BF),
            jax.ShapeDtypeStruct((4, nz * tokens, att), BF),
            jax.ShapeDtypeStruct((many, 128), F32),
            jax.ShapeDtypeStruct((ff, features), BF),
            jax.ShapeDtypeStruct((features, ff), BF),
            jax.ShapeDtypeStruct((many, features), BF),
            jax.ShapeDtypeStruct((many, features), BF),
            jax.ShapeDtypeStruct((8, ff), F32),
        ],
        in_specs=[hbm, hbm, vmem, vmem, hbm, vmem, hbm, hbm, vmem, hbm],
        out_specs=[hbm, hbm, hbm, vmem, hbm, hbm, hbm, hbm, vmem],
        scratch_shapes=[
            pltpu.VMEM((many, features), BF),
            pltpu.VMEM((many, features), BF),
            pltpu.VMEM((3, features, att), BF),
            pltpu.VMEM((att, features), BF),
            pltpu.VMEM((features, ff), BF),
            pltpu.VMEM((ff, features), BF),
            pltpu.VMEM((nz, 4, tokens, att), BF),
            pltpu.VMEM((many, ff), BF),
            pltpu.VMEM((many, ff), BF),
            pltpu.VMEM((2, tokens, features), BF),
            pltpu.SemaphoreType.DMA((2, 2, 14)),
            pltpu.SemaphoreType.DMA((2, 2, 4)),
            pltpu.SemaphoreType.DMA((6,)),
            pltpu.SemaphoreType.DMA((4,)),
            pltpu.SemaphoreType.DMA((2,)),
        ],
        compiler_params=pltpu.CompilerParams(
            collective_id=2, has_side_effects=True, vmem_limit_bytes=60 << 20
        ),
        cost_estimate=pl.CostEstimate(
            flops=2 * many * features * (6 * ff + 4 * att), bytes_accessed=100 << 20, transcendentals=0
        ),
        name="front",
    )(*operands)


MIDDLE_CHUNK = 1 << 19
TAIL_CHUNK = 1 << 18


def add_rows(target, one, two):
    @pl.loop(0, target.shape[0], step=16)
    def _(r):
        at = pl.ds(pl.multiple_of(r, 16), 16)
        target[at] = (one[at].astype(F32) + two[at].astype(F32)).astype(BF)


def chain_chunks(shapes, chunk_bytes):
    chunks, sizes = [], []
    for a, (rows, columns) in enumerate(shapes):
        size = math.gcd(rows, 1 << (chunk_bytes // (2 * columns)).bit_length() - 1)
        sizes.append(size)
        chunks += [(a, first, size) for first in range(0, rows, size)]
    return chunks, sizes


class Chain:
    def __init__(self, shapes, own, outs, landed, crossed, stage, sems, stage_sem, keep_sem):
        self.chunks = chain_chunks(shapes, MIDDLE_CHUNK if stage else TAIL_CHUNK)[0]
        self.own, self.outs, self.landed, self.crossed = own, outs, landed, crossed
        self.stage, self.sems, self.stage_sem, self.keep_sem = stage, sems, stage_sem, keep_sem
        self.n = len(self.chunks)
        self.x, self.z = lax.axis_index("dp"), lax.axis_index("blk")
        self.at_end = (self.z == 0) | (self.z == 3)
        self.inner = jnp.where(self.z == 0, 1, 2)
        self.outer = jnp.where(self.z == 1, 0, 3)

    @staticmethod
    def scratch(shapes, staged, chunk):
        chunks, sizes = chain_chunks(shapes, chunk)
        full = [pltpu.VMEM(s, BF) for s in shapes]
        stages = [pltpu.VMEM((3, n, s[1]), BF) for n, s in zip(sizes, shapes)] if staged else []
        return full * 2 + stages + [
            pltpu.SemaphoreType.DMA((8, len(chunks))),
            pltpu.SemaphoreType.DMA((3,)),
            pltpu.SemaphoreType.DMA((len(chunks),)),
        ]

    def send(self, kind, c, src, dst, device):
        return pltpu.make_async_remote_copy(
            src, dst, self.sems.at[2 * kind, c], self.sems.at[2 * kind + 1, c],
            device_id=device, device_id_type=MESH,
        )

    def rows(self, refs, c):
        a, first, size = self.chunks[c]
        return refs[a].at[pl.ds(first, size)]

    def final(self, c, half):
        a, first, size = self.chunks[c]
        return self.outs[a].at[half, pl.ds(first, size)]

    def go_in(self, c):
        return self.send(0, c, self.rows(self.own, c), self.rows(self.landed, c), {"blk": self.inner})

    def go_mid(self, c):
        return self.send(1, c, self.rows(self.landed, c), self.rows(self.crossed, c), {"blk": 3 - self.z})

    def go_out(self, c):
        return self.send(2, c, self.rows(self.crossed, c), self.final(c, self.x), {"blk": self.outer})

    def arrive_out(self, c):
        return self.send(2, c, self.final(c, self.x), self.final(c, self.x), {"blk": self.inner})

    def go_x(self, c, end):
        src = self.final(c, self.x) if end else self.rows(self.crossed, c)
        return self.send(3, c, src, self.final(c, self.x), {"dp": 1 - self.x})

    def arrive_x(self, c):
        ref = self.final(c, 1 - self.x)
        return self.send(3, c, ref, ref, {"dp": 1 - self.x})

    def load(self, c):
        a = self.chunks[c][0]
        return pltpu.make_async_copy(
            self.rows(self.own, c), self.stage[a].at[c % 3], self.stage_sem.at[c % 3]
        )

    def keep(self, c):
        return pltpu.make_async_copy(
            self.rows(self.crossed, c), self.final(c, self.x), self.keep_sem.at[c]
        )

    END_LAG = 3
    MID_LAG = 1

    @property
    def steps(self):
        return self.n + self.END_LAG

    def begin(self):
        @pl.when(self.at_end)
        def _():
            for c in range(min(2, self.n)):
                self.go_in(c).start()

        if self.stage:

            @pl.when(jnp.logical_not(self.at_end))
            def _():
                for c in range(min(2, self.n)):
                    self.load(c).start()

    def step(self, c):
        @pl.when(self.at_end)
        def _():
            if c < self.n:
                self.go_in(c).wait_send()
                if c + 2 < self.n:
                    self.go_in(c + 2).start()
            d = c - self.END_LAG
            if 0 <= d < self.n:
                self.arrive_out(d).wait_recv()
                if d >= 2:
                    self.go_x(d - 2, True).wait_send()
                self.go_x(d, True).start()

        if c < self.n + self.MID_LAG:

            @pl.when(jnp.logical_not(self.at_end))
            def _():
                if c < self.n:
                    if self.stage:
                        if c + 2 < self.n:
                            self.load(c + 2).start()
                        self.load(c).wait()
                        mine = self.stage[self.chunks[c][0]].at[c % 3]
                    else:
                        mine = self.rows(self.own, c)
                    self.go_in(c).wait_recv()
                    add_rows(self.rows(self.landed, c), self.rows(self.landed, c), mine)
                    self.go_mid(c).start()
                d = c - self.MID_LAG
                if 0 <= d < self.n:
                    self.go_mid(d).wait_recv()
                    add_rows(self.rows(self.crossed, d), self.rows(self.crossed, d), self.rows(self.landed, d))
                    self.go_out(d).start()
                    self.go_x(d, False).start()
                    self.keep(d).start()

    def finish(self):
        @pl.when(self.at_end)
        def _():
            for c in range(max(0, self.n - 2), self.n):
                self.go_x(c, True).wait_send()

        @pl.when(jnp.logical_not(self.at_end))
        def _():
            for c in range(self.n):
                self.go_mid(c).wait_send()
                self.go_out(c).wait_send()
                self.go_x(c, False).wait_send()
                self.keep(c).wait()

        for c in range(self.n):
            self.arrive_x(c).wait_recv()


def greet(devices):
    barrier = pltpu.get_barrier_semaphore()
    for device in devices:
        pl.semaphore_signal(barrier, inc=1, device_id=device, device_id_type=MESH)
    pl.semaphore_wait(barrier, len(devices))


def chain_kernel(shapes, *refs):
    count = len(shapes)
    own, outs, landed, crossed, stage = (refs[i * count : (i + 1) * count] for i in range(5))
    x, z = lax.axis_index("dp"), lax.axis_index("blk")
    greet([{"dp": 1 - x}] + [{"blk": flip(z, m)} for m in (1, 2, 3)])
    work = Chain(shapes, own, outs, landed, crossed, stage, *refs[5 * count :])
    work.begin()
    for c in range(work.steps):
        work.step(c)
    work.finish()


def chain(arrays, collective_id):
    shapes = [a.shape for a in arrays]
    hbm = pl.BlockSpec(memory_space=pl.ANY)
    return pl.pallas_call(
        functools.partial(chain_kernel, shapes),
        out_shape=[jax.ShapeDtypeStruct((2,) + s, BF) for s in shapes],
        in_specs=[hbm] * len(arrays),
        out_specs=[hbm] * len(arrays),
        scratch_shapes=Chain.scratch(shapes, True, MIDDLE_CHUNK),
        compiler_params=pltpu.CompilerParams(
            collective_id=collective_id, has_side_effects=True, vmem_limit_bytes=60 << 20
        ),
        cost_estimate=pl.CostEstimate(
            flops=0, bytes_accessed=sum(a.size for a in arrays) * 60, transcendentals=0
        ),
        name="weight_sums",
    )(*arrays)


def turn(source, cos_t, sin_t):
    half = ROT // 2
    front_half, back_half = source[:half], source[half:ROT]
    return jnp.concatenate(
        [front_half * cos_t - back_half * sin_t, back_half * cos_t + front_half * sin_t, source[ROT:]], axis=0
    )


def attention_heads(
    first_head, heads, tile, land, cos_ref, sin_ref, start_ref, out, q_t, k_t, v_t, g_t, q_n, k_n, probs, dk_acc, dv_acc,
    between,
):
    total = land.shape[1]
    steps = total // tile
    scale = HD**-0.5
    hs = range(heads)

    def lanes(h):
        return slice((first_head + h) * HD, (first_head + h + 1) * HD)

    @pl.loop(0, steps)
    def _(i):
        place = pl.ds(pl.multiple_of(i * tile, tile), tile)
        cos_t, sin_t = cos_ref[:, place], sin_ref[:, place]
        for h in hs:
            x = turn(land[0, place, lanes(h)].astype(F32).T, cos_t, sin_t) * scale
            q_t[h, :, place] = x.astype(BF)
            q_n[h, place, :] = x.T.astype(BF)
            x = turn(land[1, place, lanes(h)].astype(F32).T, cos_t, sin_t)
            k_t[h, :, place] = x.astype(BF)
            k_n[h, place, :] = x.T.astype(BF)
            v_t[h, :, place] = land[2, place, lanes(h)].astype(F32).T.astype(BF)
            g_t[h, :, place] = land[3, place, lanes(h)].astype(F32).T.astype(BF)
            dk_acc[h, place, :] = jnp.zeros((tile, HD), F32)
            dv_acc[h, place, :] = jnp.zeros((tile, HD), F32)

    def one_tile(i):
        qs = pl.ds(pl.multiple_of(i * tile, tile), tile)
        start = start_ref[:, qs]
        queries = [q_t[h, :, qs] for h in hs]
        queries_n = [q_n[h, qs, :] for h in hs]
        cots = [g_t[h, :, qs] for h in hs]
        cots_n = [land[3, qs, lanes(h)] for h in hs]
        key_at = lax.broadcasted_iota(jnp.int32, (tile, tile), 0)
        query_at = lax.broadcasted_iota(jnp.int32, (tile, tile), 1)

        def score(j, tops, diagonal):
            first = pl.multiple_of(j * tile, tile)
            allowed = key_at >= (start - first)
            if diagonal:
                allowed = allowed & (key_at <= query_at)
            result = []
            for h in hs:
                s = dot32(k_n[h, pl.ds(first, tile), :], queries[h])
                s = jnp.where(allowed, s, NEGATIVE)
                probs[h, pl.ds(first, tile), :] = s
                result.append(jnp.maximum(tops[h], jnp.max(s, axis=0, keepdims=True)))
            return tuple(result)

        tops = tuple(jnp.full((1, tile), NEGATIVE, F32) for _ in hs)
        tops = lax.fori_loop(0, i, lambda j, c: score(j, c, False), tops)
        tops = score(i, tops, True)

        def mix(j, carry):
            sums, mixed = carry
            ks = pl.ds(pl.multiple_of(j * tile, tile), tile)
            new_sums, new_mixed = [], []
            for h in hs:
                p = jnp.exp(probs[h, ks, :] - tops[h])
                probs[h, ks, :] = p
                new_sums.append(sums[h] + jnp.sum(p, axis=0, keepdims=True))
                new_mixed.append(mixed[h] + dot32(v_t[h, :, ks], p.astype(BF)))
            return tuple(new_sums), tuple(new_mixed)

        zeros = tuple(jnp.zeros((1, tile), F32) for _ in hs)
        wide_zeros = tuple(jnp.zeros((HD, tile), F32) for _ in hs)
        sums, mixed = lax.fori_loop(0, i + 1, mix, (zeros, wide_zeros))
        inverse = [1.0 / sums[h] for h in hs]
        mixed = [mixed[h] * inverse[h] for h in hs]
        delta = [jnp.sum(mixed[h] * cots[h].astype(F32), axis=0, keepdims=True) for h in hs]

        def back(j, carry):
            ks = pl.ds(pl.multiple_of(j * tile, tile), tile)
            result = []
            for h in hs:
                p = probs[h, ks, :] * inverse[h]
                dp = dot32(land[2, ks, lanes(h)], cots[h])
                ds = (p * (dp - delta[h])).astype(BF)
                dv_acc[h, ks, :] += dot32(p.astype(BF), cots_n[h])
                dk_acc[h, ks, :] += dot32(ds, queries_n[h])
                result.append(carry[h] + dot32(k_t[h, :, ks], ds))
            return tuple(result)

        dq = lax.fori_loop(0, i + 1, back, wide_zeros)
        cos_t, sin_t = cos_ref[:, qs], sin_ref[:, qs]
        for h in hs:
            out[i, 0, :, lanes(h)] = turn(dq[h] * scale, cos_t, -sin_t).T.astype(BF)
            out[i, 3, :, lanes(h)] = mixed[h].T.astype(BF)

    @pl.loop(0, steps)
    def _(i):
        one_tile(i)
        between(i)

    @pl.loop(0, steps)
    def _(i):
        place = pl.ds(pl.multiple_of(i * tile, tile), tile)
        cos_t, sin_t = cos_ref[:, place], sin_ref[:, place]
        for h in hs:
            out[i, 1, :, lanes(h)] = turn(dk_acc[h, place, :].T, cos_t, -sin_t).T.astype(BF)
            out[i, 2, :, lanes(h)] = dv_acc[h, place, :].astype(BF)


def middle_kernel(shapes, heads, tokens, schedule, *refs):
    count = len(shapes)
    land, cos_ref, sin_ref, start_ref = refs[:4]
    own, refs = refs[4 : 4 + count], refs[4 + count :]
    home, refs = refs[0], refs[1:]
    outs, refs = refs[:count], refs[count:]
    scratch, refs = refs[:10], refs[10:]
    home_sems, home_keep, refs = refs[0], refs[1], refs[2:]
    landed, crossed, stage = (refs[i * count : (i + 1) * count] for i in range(3))
    out = scratch[0]
    nz, att = out.shape[0], out.shape[3]
    groups = att // (heads * HD)
    x, z = lax.axis_index("dp"), lax.axis_index("blk")
    greet([{"dp": 1 - x}] + [{"blk": flip(z, m)} for m in range(1, nz)])
    work = Chain(shapes, own, outs, landed, crossed, stage, *refs[3 * count :])
    work.begin()

    def lanes(p):
        return pl.ds(p * heads * HD, heads * HD)

    def back(p, m):
        src = out.at[flip(z, m), :, :, lanes(p)]
        dst = home.at[:, z, :, lanes(p)]
        if m == 0:
            return pltpu.make_async_copy(src, dst, home_keep.at[p])
        return pltpu.make_async_remote_copy(
            src, dst, home_sems.at[0, p, m], home_sems.at[1, p, m], device_id={"blk": flip(z, m)}, device_id_type=MESH
        )

    def arrived(p, m):
        ref = home.at[:, flip(z, m), :, lanes(p)]
        return pltpu.make_async_remote_copy(
            ref, ref, home_sems.at[0, p, m], home_sems.at[1, p, m], device_id={"blk": flip(z, m)}, device_id_type=MESH
        )

    done = 0
    for p in range(groups):
        plan = schedule[p] if p < len(schedule) else ()
        first = done
        done += sum(plan)

        def between(i, plan=plan, first=first):
            at = first
            for tile, steps in enumerate(plan):
                if steps:

                    @pl.when(i == tile)
                    def _(at=at, steps=steps):
                        for c in range(at, at + steps):
                            work.step(c)

                at += steps

        attention_heads(p * heads, heads, tokens, land, cos_ref, sin_ref, start_ref, *scratch, between)
        for m in (2, 3, 1, 0):
            back(p, m).start()
    for c in range(done, work.steps):
        work.step(c)
    work.finish()
    for p in range(groups):
        for m in range(nz):
            if m == 0:
                back(p, m).wait()
            else:
                back(p, m).wait_send()
                arrived(p, m).wait_recv()


def middle(land, cos_t, sin_t, start, arrays, tokens, schedule):
    _, total, att = land.shape
    nz = total // tokens
    heads = min(2, att // HD)
    groups = att // (heads * HD)
    shapes = [a.shape for a in arrays]
    hbm = pl.BlockSpec(memory_space=pl.ANY)
    vmem = pl.BlockSpec(memory_space=pltpu.VMEM)
    results = pl.pallas_call(
        functools.partial(middle_kernel, shapes, heads, tokens, schedule),
        out_shape=[jax.ShapeDtypeStruct((4, nz, tokens, att), BF)]
        + [jax.ShapeDtypeStruct((2,) + s, BF) for s in shapes],
        in_specs=[vmem] * 4 + [hbm] * len(arrays),
        out_specs=[hbm] * (1 + len(arrays)),
        scratch_shapes=[pltpu.VMEM((nz, 4, tokens, att), BF)]
        + [pltpu.VMEM((heads, HD, total), BF)] * 4
        + [pltpu.VMEM((heads, total, HD), BF)] * 2
        + [pltpu.VMEM((heads, total, tokens), F32)]
        + [pltpu.VMEM((heads, total, HD), F32)] * 2
        + [pltpu.SemaphoreType.DMA((2, groups, nz)), pltpu.SemaphoreType.DMA((groups,))]
        + Chain.scratch(shapes, True, MIDDLE_CHUNK),
        compiler_params=pltpu.CompilerParams(
            collective_id=3, has_side_effects=True, vmem_limit_bytes=60 << 20
        ),
        cost_estimate=pl.CostEstimate(
            flops=12 * (att // HD) * total * total * HD * 4, bytes_accessed=1 << 28, transcendentals=0
        ),
        name="middle",
    )(land, cos_t, sin_t, start, *arrays)
    return results[0], results[1:]


def tail_kernel(
    shapes, split, rows, tokens, home, g_ref, normed_ref, wq_ref, wo_ref, branch_ff, dnorm_ff,
    out_sum, qkv_sum, branch_o, dnorm_o,
    stream, hcat, wcat, wo, dwo, dwq, give, take, take_y, take_x, tile_buf,
    load_sems, stream_sems, tile_sems, scatter_sems, *chain_refs,
):
    x, z, t = lax.axis_index("dp"), lax.axis_index("blk"), lax.axis_index("tensor")
    many, four = hcat.shape
    att = four // 4
    features = wo.shape[1]
    half = many // 2
    width = features // 4
    core, y = t % 2, t // 2
    peers = {"x": {"dp": 1 - x}, "y": {"tensor": flip(t, 2)}, "c": {"tensor": flip(t, 1)}}
    loads = [
        pltpu.make_async_copy(home.at[i], hcat.at[:, pl.ds(i * att, att)], load_sems.at[i]) for i in range(4)
    ] + [
        pltpu.make_async_copy(
            wq_ref.at[i, :, pl.ds(pl.multiple_of(x * att, 128), att)] if split else wq_ref.at[i],
            wcat.at[:, pl.ds(i * att, att)],
            load_sems.at[4 + i],
        )
        for i in range(3)
    ] + [pltpu.make_async_copy(wo_ref.at[pl.ds(x * att, att)] if split else wo_ref, wo, load_sems.at[7])]

    def streamed(k):
        source = g_ref if k < 2 else normed_ref
        return pltpu.make_async_copy(
            source.at[:, pl.ds((k % 2) * (features // 2), features // 2)], stream.at[k % 2], stream_sems.at[k % 2]
        )

    loads[3].start()
    streamed(0).start()
    streamed(1).start()
    for load in loads[:3] + loads[4:]:
        load.start()
    greet([{"blk": flip(z, m)} for m in (1, 2, 3)] + list(peers.values()))

    tn_dims = (((0,), (0,)), ((), ()))
    nt_dims = (((1,), (1,)), ((), ()))
    general = functools.partial(lax.dot_general, preferred_element_type=F32)
    loads[3].wait()
    for k in range(2):
        streamed(k).wait()

        @pl.loop(0, features // 1024)
        def _(j, k=k):
            columns = pl.ds(pl.multiple_of(j * 512, 512), 512)
            value = general(hcat[:, 3 * att :], stream[k, :, columns], tn_dims)
            dwo[:, pl.ds(pl.multiple_of(k * (features // 2) + j * 512, 512), 512)] = value.astype(BF)

        streamed(k + 2).start()
    for load in loads[:3]:
        load.wait()
    for k in range(2):
        streamed(k + 2).wait()

        @pl.loop(0, features // 512)
        def _(j, k=k):
            f = pl.ds(pl.multiple_of(j * 256, 256), 256)
            value = general(stream[k, :, f], hcat[:, : 3 * att], tn_dims).astype(BF)
            for i in range(3):
                at = pl.multiple_of(i * features + k * (features // 2) + j * 256, 256)
                dwq[pl.ds(at, 256), :] = value[:, i * att : (i + 1) * att]

    work = Chain(shapes, [dwo, dwq], [out_sum, qkv_sum], chain_refs[:2], chain_refs[2:4], None, *chain_refs[4:])
    work.begin()

    for load in loads[4:]:
        load.wait()

    def share(which, of_core, target, plus):
        source = branch_ff if which == 0 else dnorm_ff
        blocks = many // tokens

        def columns(v):
            return pl.ds(pl.multiple_of((2 * v + of_core) * width, width), width)

        def fetch(k):
            at = pl.ds(pl.multiple_of((k % blocks) * tokens, tokens), tokens)
            return pltpu.make_async_copy(source.at[at, columns(k // blocks)], tile_buf.at[k % 2], tile_sems.at[k % 2])

        fetch(0).start()

        @pl.loop(0, 2 * blocks)
        def _(k):
            @pl.when(k + 1 < 2 * blocks)
            def _():
                fetch(k + 1).start()

            fetch(k).wait()
            v = k // blocks
            at = pl.ds(pl.multiple_of((k % blocks) * tokens, tokens), tokens)
            value = tile_buf[k % 2].astype(F32)
            if which == 0:
                value = value + dot32(hcat[at, 3 * att :], wo[:, columns(v)])
            else:
                value = value + general(hcat[at, : 3 * att], wcat[columns(v), :], nt_dims)
            if plus:
                value = value + target[v, at, :].astype(F32)
            target[v, at, :] = value.astype(BF)

    def remote(which, stage, src, dst, to):
        return pltpu.make_async_remote_copy(
            src, dst, scatter_sems.at[0, which, stage], scatter_sems.at[1, which, stage],
            device_id=peers[to], device_id_type=MESH,
        )

    def over_core(which):
        return remote(which, 0, give, take.at[which], "c")

    def over_y(which):
        return remote(which, 1, take.at[which, 1 - y], take_y.at[which], "y")

    def over_x(which):
        return remote(which, 2, take_y.at[which, pl.ds((1 - x) * half, half)], take_x.at[which], "x")

    def stage_one(which):
        if which == 1:
            over_core(0).wait_send()
        share(which, 1 - core, give, False)
        over_core(which).start()

    def stage_two(which):
        over_core(which).wait_recv()
        share(which, core, take.at[which], True)
        over_y(which).start()

    def stage_three(which):
        over_y(which).wait_recv()

        @pl.loop(0, many // 256)
        def _(i):
            at = pl.ds(pl.multiple_of(i * 256, 256), 256)
            take_y[which, at, :] = (take_y[which, at, :].astype(F32) + take[which, y, at, :].astype(F32)).astype(BF)

        over_x(which).start()

    def stage_four(which):
        over_x(which).wait_recv()
        target = (branch_o, dnorm_o)[which]

        @pl.loop(0, half // 256)
        def _(i):
            at = pl.ds(pl.multiple_of(i * 256, 256), 256)
            mine = pl.ds(pl.multiple_of(x * half + i * 256, 256), 256)
            target[at, :] = take_x[which, at, :].astype(F32) + take_y[which, mine, :].astype(F32)

    stages = {
        0: [(stage_one, 0)], 1: [(stage_one, 1)], 2: [(stage_two, 0)], 3: [(stage_two, 1)],
        11: [(stage_three, 0)], 15: [(stage_three, 1)], 16: [(stage_four, 0)],
    }
    last = [(stage_three, 0), (stage_three, 1), (stage_four, 0), (stage_four, 1)]
    for c in range(work.steps):
        for stage, which in stages.get(c, ()):
            stage(which)
            if (stage, which) in last:
                last.remove((stage, which))
        work.step(c)
    for stage, which in last:
        stage(which)
    work.finish()
    over_core(1).wait_send()
    for which in range(2):
        over_y(which).wait_send()
        over_x(which).wait_send()


def tail(split, rows, tokens, home, cotangent, normed, wq, wo, branch_ff, dnorm_ff, att):
    many, features = normed.shape
    width = features // 4
    half = many // 2
    shapes = [(att, features), (3 * features, att)]
    hbm = pl.BlockSpec(memory_space=pl.ANY)
    vmem = pl.BlockSpec(memory_space=pltpu.VMEM)
    return pl.pallas_call(
        functools.partial(tail_kernel, shapes, split, rows, tokens),
        out_shape=[jax.ShapeDtypeStruct((2,) + s, BF) for s in shapes]
        + [jax.ShapeDtypeStruct((half, width), F32)] * 2,
        in_specs=[hbm] * 7,
        out_specs=[hbm] * 2 + [vmem] * 2,
        scratch_shapes=[
            pltpu.VMEM((2, many, features // 2), BF),
            pltpu.VMEM((many, 4 * att), BF),
            pltpu.VMEM((features, 3 * att), BF),
            pltpu.VMEM((att, features), BF),
            pltpu.VMEM((att, features), BF),
            pltpu.VMEM((3 * features, att), BF),
            pltpu.VMEM((2, many, width), BF),
            pltpu.VMEM((2, 2, many, width), BF),
            pltpu.VMEM((2, many, width), BF),
            pltpu.VMEM((2, half, width), BF),
            pltpu.VMEM((2, tokens, width), BF),
            pltpu.SemaphoreType.DMA((8,)),
            pltpu.SemaphoreType.DMA((2,)),
            pltpu.SemaphoreType.DMA((2,)),
            pltpu.SemaphoreType.DMA((2, 2, 3)),
        ]
        + Chain.scratch(shapes, False, TAIL_CHUNK),
        compiler_params=pltpu.CompilerParams(
            collective_id=4, has_side_effects=True, vmem_limit_bytes=62 << 20
        ),
        cost_estimate=pl.CostEstimate(flops=30 << 30, bytes_accessed=1 << 28, transcendentals=0),
        name="tail",
    )(home, cotangent, normed, wq, wo, branch_ff, dnorm_ff)


def widen(source, by_columns):
    _, rows, columns = source.shape
    size = min(rows, (1 << 18) // columns)

    def body(source_ref, out_ref):
        out_ref[...] = source_ref[0].astype(F32)

    if by_columns and columns % 128:
        both = jnp.concatenate([source[0], source[1]], axis=1)
        return both.astype(F32)
    shape = (rows, 2 * columns) if by_columns else (2 * rows, columns)
    steps = rows // size
    out_map = (lambda i, h: (i, h)) if by_columns else (lambda i, h: (h * steps + i, 0))
    return pl.pallas_call(
        body,
        out_shape=jax.ShapeDtypeStruct(shape, F32),
        grid=(steps, 2),
        in_specs=[pl.BlockSpec((1, size, columns), lambda i, h: (h, i, 0))],
        out_specs=pl.BlockSpec((size, columns), out_map),
        compiler_params=pltpu.CompilerParams(vmem_limit_bytes=32 << 20),
        cost_estimate=pl.CostEstimate(flops=0, bytes_accessed=source.size * 6, transcendentals=0),
        name="widen",
    )(source)


def scatter_sum(share):
    whole = lax.psum_scatter(share.astype(BF), "dp", scatter_dimension=0, tiled=True)
    return lax.psum_scatter(whole, "tensor", scatter_dimension=2, tiled=True).astype(F32)


def butterfly(value, axes):
    for axis, size in axes:
        mask = 1
        while mask < size:
            value = value + swap(value, axis, size, mask)
            mask *= 2
    return value


SCHEDULE = ((0, 0, 1, 1), (0, 0, 1, 1))


def local(
    nx, nz, nt, block_input, segment_ids, layer_norm_gain, layer_norm_bias, qkv_weight, qkv_bias, out_weight, out_bias,
    up_weight, up_bias, down_weight, down_bias, grad_output,
):
    rows, tokens, width = block_input.shape
    all_rows = nx * rows
    features = nt * width
    many = all_rows * tokens
    x, z, t = lax.axis_index("dp"), lax.axis_index("blk"), lax.axis_index("tensor")
    att = qkv_weight.shape[2] // nx
    ff = up_weight.shape[1] // nx

    gather = nt == 4 and nx == 2
    split = att % 128 == 0
    qkv_whole = jnp.transpose(qkv_weight, (1, 0, 2))
    qkv_half = lax.dynamic_slice_in_dim(qkv_whole, x * att, att, 2)
    qkv_half_bias = lax.dynamic_slice_in_dim(qkv_bias, x * att, att, 1)
    out_half = lax.dynamic_slice_in_dim(out_weight, x * att, att, 0)
    up_half_bias = lax.dynamic_slice_in_dim(up_bias, x * ff, ff, 0)
    if split:
        weights = [qkv_whole, out_weight, up_weight, down_weight]
    else:
        up_half = lax.dynamic_slice_in_dim(up_weight, x * ff, ff, 1)
        down_half = lax.dynamic_slice_in_dim(down_weight, x * ff, ff, 0)
        weights = [qkv_half, out_half, up_half, down_half]

    segments = lax.ppermute(segment_ids, "dp", [(0, 1), (1, 0)])
    segments = jnp.where(z // rows == x, segment_ids, segments)
    segments = lax.dynamic_slice_in_dim(segments, z % rows, 1, 0)
    length = segments.shape[1]
    places = jnp.arange(length, dtype=jnp.int32)[None]
    changed = jnp.concatenate(
        [jnp.ones((1, 1), dtype=bool), segments[:, 1:] != segments[:, :-1]], axis=1
    )
    start = lax.cummax(jnp.where(changed, places, 0), axis=1)
    half_rot = ROT // 2
    frequency = jnp.exp(jnp.arange(half_rot).astype(F32) * (-2.0 / ROT) * ROPE_LOG_BASE)
    angles = frequency[:, None] * (places - start).astype(F32)
    cos_t, sin_t = jnp.cos(angles), jnp.sin(angles)

    if gather:
        sources = [block_input.reshape(rows * tokens, width), grad_output.reshape(rows * tokens, width)]
    else:
        sources = [lax.all_gather(a, "tensor", axis=2, tiled=True) for a in (block_input, grad_output)]
        sources = [lax.all_gather(a, "dp", axis=0, tiled=True).reshape(many, features) for a in sources]
    normed, cotangent, land, stats, down_part, up_part, branch_ff, d_normed_ff, up_bias_part = front(
        gather, split, rows, tokens, nz, many, features, att, ff,
        [
            *sources, layer_norm_gain.reshape(1, features), layer_norm_bias.reshape(1, features), weights[0],
            qkv_half_bias.reshape(3, 1, att), weights[1], weights[2], up_half_bias.reshape(1, ff), weights[3],
        ],
    )
    home, (down_sum, up_sum) = middle(
        land, cos_t, sin_t, start, [down_part, up_part], tokens, SCHEDULE
    )
    home = home.reshape(4, many, att)
    qkv_bias_part = jnp.sum(home[:3].astype(F32), axis=1)
    up_bias_part = up_bias_part[0]
    if gather:
        out_sum, qkv_sum, branch, d_normed = tail(
            split, rows, tokens, home, cotangent, normed, weights[0], weights[1], branch_ff, d_normed_ff, att
        )
        branch = branch.reshape(rows, tokens, width)
        d_normed = d_normed.reshape(rows, tokens, width)
    else:
        branch = branch_ff.astype(F32) + dot32(home[3], out_half)
        d_normed = d_normed_ff.astype(F32)
        for i in range(3):
            d_normed = d_normed + dot32(home[i], qkv_half[i].T)
        branch = scatter_sum(branch.reshape(all_rows, tokens, features))
        d_normed = scatter_sum(d_normed.reshape(all_rows, tokens, features))
        qkv_part = jnp.concatenate([dot32(normed.T, home[i]).astype(BF) for i in range(3)])
        out_sum, qkv_sum = chain([dot32(home[3].T, cotangent).astype(BF), qkv_part], 1)

    block_output = (block_input.astype(F32) + (branch + out_bias + down_bias)).astype(BF)

    gain = lax.dynamic_slice_in_dim(layer_norm_gain, t * width, width, 0)
    stats = lax.dynamic_slice_in_dim(stats, x * rows * tokens, rows * tokens, 0).reshape(rows, tokens, 128)
    own_mean, own_inverse = stats[..., :1], stats[..., 64:65]
    xhat = (block_input.astype(F32) - own_mean) * own_inverse
    scaled = d_normed * gain
    moments = jnp.stack([jnp.sum(scaled, axis=-1), jnp.sum(scaled * xhat, axis=-1)])
    moments = butterfly(moments, [("tensor", nt)]) / features
    first, second = moments[0][..., None], moments[1][..., None]
    input_grad = (
        grad_output.astype(F32) + own_inverse * (scaled - first - xhat * second)
    ).astype(BF)

    def spread(part, whole):
        shape = part.shape[:-1] + (whole,)
        at = (0,) * (part.ndim - 1) + (x * part.shape[-1],)
        return lax.dynamic_update_slice(jnp.zeros(shape, F32), part, at)

    small = [
        jnp.sum(d_normed * xhat, axis=(0, 1)),
        jnp.sum(d_normed, axis=(0, 1)),
        jnp.sum(grad_output.astype(F32), axis=(0, 1)),
        spread(up_bias_part, nx * ff),
        spread(qkv_bias_part, nx * att).reshape(-1),
    ]
    packed = butterfly(jnp.concatenate(small), [("dp", nx), ("blk", nz)])
    gain_grad, shift_grad, bias_grad = (packed[i * width : (i + 1) * width] for i in range(3))
    up_bias_grad = packed[3 * width : 3 * width + nx * ff]
    qkv_bias_grad = packed[3 * width + nx * ff :].reshape(3, nx * att)

    down_grad = widen(down_sum, False)
    up_grad = widen(up_sum, True)
    out_grad = widen(out_sum, False)
    qkv_grad = widen(qkv_sum, True).reshape(3, features, nx * att)
    qkv_grad = jnp.transpose(qkv_grad, (1, 0, 2))
    return (
        block_output, input_grad, gain_grad, shift_grad, qkv_grad, qkv_bias_grad, out_grad, bias_grad, up_grad,
        up_bias_grad, down_grad, bias_grad,
    )


def solution(mesh):
    in_specs = (
        P("dp", "blk", "tensor"), P("dp", None), P(), P(), P(None, None, "tensor"), P(None, "tensor"), P("tensor", None),
        P("tensor"), P(None, "tensor"), P("tensor"), P("tensor", None), P("tensor"), P("dp", "blk", "tensor"),
    )
    out_specs = (
        P("dp", "blk", "tensor"), P("dp", "blk", "tensor"), P("tensor"), P("tensor"), P(None, None, "tensor"),
        P(None, "tensor"), P("tensor", None), P("tensor"), P(None, "tensor"), P("tensor"), P("tensor", None), P("tensor"),
    )
    body = functools.partial(local, mesh.shape["dp"], mesh.shape["blk"], mesh.shape["tensor"])
    return jax.shard_map(body, mesh=mesh, in_specs=in_specs, out_specs=out_specs, check_vma=False)
```

time: 1100 us -> 723 us (0.66)
  Pallas kernels: 430 us -> 685 us
  local copies, waits for them, and re-layouts: 228 us -> 8.24 us
  matrix products: 172 us -> 0 us
  waiting for transfers between devices: 152 us -> 11.2 us
  other arithmetic: 67.7 us -> 11.7 us
  starting transfers between devices: 42.5 us -> 4.33 us
    pallas_call x4 -> x7, Pallas kernels: 430 us -> 685 us  [the longest x1 324 us: middle(): pl.pallas_call(functools.partial(middle_kernel, shapes, heads, tokens, sc...]
    dot_general x23 -> x0, matrix products: 172 us -> none  [the longest x1 19.5 us: local(): d_hidden = (dot32(cotangent, down_half.T) * slope).astype(BF)]
    ppermute x45 -> x5, waiting for transfers between devices: 152 us -> 11.2 us  [swap(): return lax.ppermute(value, axis, [(i, i ^ mask) for i in range(size)])]
    unnamed x165 -> x33, local copies, waits for them, and re-layouts: 78.4 us -> 0.84 us
    convert_element_type x9 -> x0, other arithmetic: 53 us -> none  [the longest x2 11.8 us: scatter_sum(): (make(core) + other.astype(F32)).astype(BF)]
    convert_element_type x5 -> x0, local copies, waits for them, and re-layouts: 46.9 us -> none  [the longest x1 17.8 us: local(): up_grad = jnp.swapaxes(up_sum, 0, 1).reshape(features, nx * ff).astype(F32)]
    ppermute x45 -> x5, starting transfers between devices: 41 us -> 1.33 us  [swap(): return lax.ppermute(value, axis, [(i, i ^ mask) for i in range(size)])]
    dynamic_update_slice x22 -> x0, local copies, waits for them, and re-layouts: 21.3 us -> none  [the longest x16 21.1 us: gather_all(): out = lax.dynamic_update_slice(out, block, at)]
  transfers between devices with their start and end apart: 46 -> 6, of which waited for: 12 -> 4; matrix products, arithmetic and copies ran while one was open for 34% -> 1% of each run, Pallas kernels for 39% -> 24%
where the time goes in v2:
time: 723 us; the launch traced here: 722 us
  Pallas kernels  685 us (95%)
  other arithmetic  11.7 us (2%)
  waiting for transfers between devices  11.2 us (2%)
  local copies, waits for them, and re-layouts  8.24 us (1%)
    pallas_call x1, Pallas kernels, middle(): pl.pallas_call(functools.partial(middle_kernel, shapes, heads, tokens, sc...  324 us
    pallas_call x1, Pallas kernels, tail(): pl.pallas_call(functools.partial(tail_kernel, shapes, split, rows, tokens...  192 us
    pallas_call x1, Pallas kernels, front(): pl.pallas_call(functools.partial(front_kernel, gather, split, rows, token...  144 us
    pallas_call x4, Pallas kernels, widen(): pl.pallas_call(body, out_shape=jax.ShapeDtypeStruct(shape, F32), grid=(st...  26.4 us
  transfers between devices with their start and end apart: 6, of which 4 were waited for; matrix products, arithmetic and copies ran while one was open for 1% of the time, Pallas kernels for 24%

profile of v2, /device:TPU:0, one launch (start us, length us, event | category | flops | bytes accessed | tf_op | source)
XLA Modules:
  0.0 721.9 jit_solution(3489224529623887421)
XLA Ops:
  0.6 0.0 copy-start
  0.7 3.0 collective-permute-start
  3.7 0.6 reshape.184.bq_ref
  4.3 1.3 dynamic_slice.16
  5.5 143.7 %front.1 = (bf16[2048,2048]{1,0:T(8,128)(2,1)}, bf16[2048,2048]{1,0:T(8,128)(2,1)}, bf16[4,2048,256]{2,1,0:T(8,128)(2,1)}, f32[2048,128]{1,0:T(8,128)}, bf16[102...) custom-call(bf16[1024,512]{1,0:T(8,128)(2,1)} %bitcast.44, ...), custom_call_target="tpu_custom_call" | custom-call | flops 60129542144 | bytes 104857600 | tf_op jit(solution)/shard_map/front/pallas_call | solution.py:340
  149.2 0.0 copy-start.7
  149.2 1.1 constant_dynamic-slice_fusion
  150.3 0.5 slice_reduce_fusion.1
  150.9 0.8 dynamic_slice.19
  151.6 0.8 slice.64
  152.4 0.3 dynamic_update_slice.6
  152.7 0.0 collective-permute-done
  152.8 0.1 slice_compare_fusion
  152.9 0.1 add_reduce_fusion
  153.0 0.3 reduce-window.6
  153.3 0.2 slice_reduce_fusion.2
  153.5 0.2 reduce-window.9
  153.7 0.1 fusion.11
  153.7 1.2 multiply_sine_fusion
  155.0 0.1 broadcast.42
  155.1 0.6 reduce_window_max.26.refs_3_
  155.7 323.8 %middle.1 = (bf16[4,4,512,256]{3,2,1,0:T(8,128)(2,1)}, bf16[2,1024,2048]{2,1,0:T(8,128)(2,1)}, bf16[2,2048,1024]{2,1,0:T(8,128)(2,1)}) custom-call(bf16[4,2048,256]{2,1,0:T(8,128)(2,1)} %get-tuple-element.28.refs_0_, f32[16,2048]{1,0:T(8,128)} %get-tuple-element.57.refs_1_, f32[16,2048]{1,0:T(8,128)} %get-tuple-element.56.refs_2_, ...), custom_call_target="tpu_custom_call" | custom-call | flops 51539607552 | bytes 268435456 | tf_op jit(solution)/shard_map/middle/pallas_call | solution.py:771
  479.5 2.4 convert_reduce_fusion
  481.9 0.0 copy-start.5
  481.9 191.6 %tail.1 = (bf16[2,256,2048]{2,1,0:T(8,128)(2,1)}, bf16[2,6144,256]{2,1,0:T(8,128)(2,1)}, f32[1024,512]{1,0:T(8,128)}, f32[1024,512]{1,0:T(8,128)}) custom-call(bf16[4,2048,256]{2,1,0:T(8,128)(2,1)} %bitcast.45, bf16[2048,2048]{1,0:T(8,128)(2,1)} %get-tuple-element.32.g_ref, bf16[2048,2048]{1,0:T(8,128)(2,1)} %get-tuple-element.33.normed_ref, ...), custom_call_target="tpu_custom_call" | custom-call | flops 32212254720 | bytes 268435456 | tf_op jit(solution)/shard_map/tail/pallas_call | solution.py:970
  673.5 2.0 fusion.13
  675.5 0.2 copy-done.4
  675.7 0.8 fusion.8
  676.5 0.2 collective-permute-start.1
  676.7 1.0 collective-permute-done.1
  677.7 1.0 collective-permute-start.2
  678.7 2.7 collective-permute-done.2
  681.5 0.0 slice-start.2
  681.5 3.9 convert_reduce_fusion.1
  685.4 0.2 collective-permute-start.3
  685.6 3.7 collective-permute-done.3
  689.3 3.8 collective-permute-done.4
  693.1 0.0 collective-permute-start.5
  693.1 0.0 slice-start.3
  693.1 6.6 widen.4
  699.7 2.4 widen.5
  702.1 8.7 %widen.6 = f32[2048,2048]{1,0:T(8,128)} custom-call(bf16[2,2048,1024]{2,1,0:T(8,128)(2,1)S(1)} %bitcast.40), custom_call_target="tpu_custom_call" | custom-call | bytes 25165824 | tf_op jit(solution)/shard_map/widen/pallas_call | solution.py:1015
  710.8 8.7 %widen.7 = f32[2048,2048]{1,0:T(8,128)} custom-call(bf16[2,1024,2048]{2,1,0:T(8,128)(2,1)S(1)} %bitcast.38), custom_call_target="tpu_custom_call" | custom-call | bytes 25165824 | tf_op jit(solution)/shard_map/widen/pallas_call | solution.py:1015
  719.5 0.0 collective-permute-done.5
  719.5 0.6 fusion.14
  720.1 0.6 slice.83
  720.7 0.6 slice.69
  721.3 0.6 copy.33
  (49 shorter events, 0.2 us)
Async XLA Ops:
  0.6 3.0 copy-start
  0.7 152.1 %collective-permute-start = (s32[2,2048]{1,0:T(2,128)}, s32[2,2048]{1,0:T(2,128)S(1)}, u32[]{:S(2)}, u32[]{:S(2)}) collective-permute-start(s32[2,2048]{1,0:T(2,128)} %param.14), channel_id=1, source_target_pairs={{0,16},{16,0},{1,17},{17,1},{2,18},{18,2},{3,19},{19,3},{4,20},{20... | collective-permute-start | bytes 49160 | tf_op jit(solution)/shard_map/ppermute | solution.py:1070
  149.2 3.5 copy-start.7
  481.9 193.6 %copy-start.5 = (bf16[2,512,512]{2,1,0:T(8,128)(2,1)S(1)}, bf16[2,512,512]{2,1,0:T(8,128)(2,1)}, u32[]{:S(2)}) copy-start(bf16[2,512,512]{2,1,0:T(8,128)(2,1)} %param.13) | copy-start | bytes 3145732
  673.4 2.2 copy-start.4
  675.7 5.8 copy-start.8
  675.7 5.8 copy-start.9
  676.5 1.2 collective-permute-start.1
  677.7 3.7 collective-permute-start.2
  681.5 11.6 %copy-start.2 = (bf16[2,6144,256]{2,1,0:T(8,128)(2,1)S(1)}, bf16[2,6144,256]{2,1,0:T(8,128)(2,1)}, u32[]{:S(2)}) copy-start(bf16[2,6144,256]{2,1,0:T(8,128)(2,1)} %get-tuple-element.40.source_ref) | copy-start | bytes 18874372
  681.5 20.6 %slice-start.2 = ((s8[8388608]{0:T(1024)(128)(4,1)}), s8[4194304]{0:T(1024)(128)(4,1)S(1)}, s32[]{:S(2)}) async-start(s8[8388608]{0:T(1024)(128)(4,1)} %bitcast.39), calls=%async_computation.2 | async-start | bytes 8388608
  685.4 3.8 collective-permute-start.3
  689.3 3.8 collective-permute-start.4
  693.1 26.4 %collective-permute-start.5 = (f32[5120]{0:T(1024)S(1)}, f32[5120]{0:T(1024)S(1)}, u32[]{:S(2)}, u32[]{:S(2)}) collective-permute-start(f32[5120]{0:T(1024)S(1)} %add.78), channel_id=1, source_target_pairs={{0,8},{4,12},{8,0},{12,4},{1,9},{5,13},{9,1},{13,5},{2,10},{6,14},... | collective-permute-start | bytes 61448 | tf_op jit(solution)/shard_map/ppermute | solution.py:23
  693.1 6.6 copy-start.3
  693.1 9.0 %slice-start.3 = ((s8[8388608]{0:T(1024)(128)(4,1)}), s8[4194304]{0:T(1024)(128)(4,1)S(1)}, s32[]{:S(2)}) async-start(s8[8388608]{0:T(1024)(128)(4,1)} %bitcast.39), calls=%async_computation.3 | async-start | bytes 8388608
  699.7 11.1 %slice-start = ((s8[8388608]{0:T(1024)(128)(4,1)}), s8[4194304]{0:T(1024)(128)(4,1)S(1)}, s32[]{:S(2)}) async-start(s8[8388608]{0:T(1024)(128)(4,1)} %bitcast.37), calls=%async_computation | async-start | bytes 8388608
  702.1 8.7 %slice-start.1 = ((s8[8388608]{0:T(1024)(128)(4,1)}), s8[4194304]{0:T(1024)(128)(4,1)S(1)}, s32[]{:S(2)}) async-start(s8[8388608]{0:T(1024)(128)(4,1)} %bitcast.37), calls=%async_computation.1 | async-start | bytes 8388608
  710.8 11.1 %copy-start.1 = (f32[3,512]{1,0:T(4,128)S(1)}, f32[3,512]{1,0:T(4,128)}, u32[]{:S(2)}) copy-start(f32[3,512]{1,0:T(4,128)} %param.18) | copy-start | bytes 18436
  720.1 1.8 copy-start.6
